TPU v7x, 256 devices: a whole 4x4x8 slice. The times are simulated.
256 devices in a mesh: group: 8 (over z), dev: 32 (over x, y, core).
Axes of the slice: x: 4, y: 4, z: 8, core: 2. Of those that a mesh axis runs over, the one named last changes fastest.
Arguments:
- embeddings: bfloat16 [229376, 768], P(('group', 'dev')), may hold values from -96 to 96
- assignment: int32 [229376, 1], P(('group', 'dev')), may hold values from 0 to 31; in each aligned block of 896 rows (0 to 895, 896 to 1791, ...) at most 56 rows name the same one
- owner_of: int32 [32], replicated, may hold values from 0 to 31, each once
- pair_on: int32 [2, 256], P(None, ('group', 'dev')), may hold values 0 or 1
Outputs:
- best_match: float32 [229376], P(('group', 'dev'))
Inputs may be any that keep to these rules, and one draw needn't show every extreme that they name: `assignment`: each storage shard of 896 rows holds at most 56 rows of any one cluster, and some shard holds exactly 56 rows of some cluster. `owner_of`: each owner index appears exactly once.
All inputs are finite; a program needn't handle non-finite values. No bound on the sum of `pair_on` on one device may be relied on, other than what follows from the above.
Results may differ from a plain program's by a relative error of at most 0.00091.
Values may be sent and summed in bfloat16 or wider, within the bound.
A program may use at most 128 MiB of HBM per device.

v0:
```python
import jax
import jax.numpy as jnp
from jax import lax
from jax.sharding import PartitionSpec as P


def passed_along(value, axis, steps):
    count = lax.axis_size(axis)
    pairs = [(source, (source + steps) % count) for source in range(count)]
    return lax.ppermute(value, axis, pairs)


def pair_maxima(left_rows, left_live, right_rows, right_live, skip_self):
    row_total = left_rows.shape[0]
    pieces = 2
    height = row_total // pieces
    right_ok = right_live[None, :] > 0
    columns = jnp.arange(right_rows.shape[0])[None, :]
    row_parts = []
    column_best = jnp.full((right_rows.shape[0],), -2.0, jnp.float32)
    for piece_id in range(pieces):
        top_rows = left_rows[piece_id * height : (piece_id + 1) * height]
        similar = lax.dot_general(
            top_rows, right_rows, (((1,), (1,)), ((), ())), preferred_element_type=jnp.float32
        )
        allowed = (left_live[piece_id * height : (piece_id + 1) * height][:, None] > 0) & right_ok
        if skip_self:
            allowed = allowed & (jnp.arange(height)[:, None] + piece_id * height != columns)
        similar = jnp.where(allowed, similar, -2.0)
        row_parts.append(jnp.max(similar, axis=1))
        column_best = jnp.maximum(column_best, jnp.max(similar, axis=0))
    return (jnp.concatenate(row_parts), column_best)


def on_device(embeddings, assignment, owner_of, pair_on):
    owner_count = owner_of.shape[0]
    capacity = 2 * embeddings.shape[0] // owner_count
    width = embeddings.shape[1]
    values = embeddings.astype(jnp.float32)
    unit_rows = (
        values * lax.rsqrt(jnp.sum(values * values, axis=1, keepdims=True) + 1e-06)
    ).astype(jnp.bfloat16)
    owner_ids = jnp.arange(owner_count, dtype=jnp.int32)
    matches = assignment[:, 0][:, None] == owner_ids[None, :]
    owners = jnp.sum(jnp.where(matches, owner_of[None, :], 0), axis=1)
    one_hot = (owners[:, None] == owner_ids[None, :]).astype(jnp.int32)
    slot_ids = jnp.sum((jnp.cumsum(one_hot, axis=0) - 1) * one_hot, axis=1)
    outbox = (
        jnp.zeros((owner_count, capacity, width), jnp.bfloat16).at[owners, slot_ids].set(unit_rows)
    )
    slot_marks = jnp.zeros((owner_count, capacity), jnp.bfloat16).at[owners, slot_ids].set(1.0)
    switches = pair_on[:, 0].astype(jnp.bfloat16)
    group_count = lax.axis_size("group")
    half_way = group_count // 2
    slot_total = owner_count * capacity
    arrived, arrived_marks = (
        lax.all_to_all(outbox, "dev", split_axis=0, concat_axis=0, tiled=True),
        lax.all_to_all(slot_marks, "dev", split_axis=0, concat_axis=0, tiled=True),
    )
    members = arrived.reshape(slot_total, width)
    present = arrived_marks.reshape(slot_total)
    leading = jnp.maximum(pair_maxima(members, present, members, present, True)[0], -1.0)
    near_rows, near_live = passed_along((members, present), "group", 1)
    near_mine, near_theirs = pair_maxima(members, present, near_rows, near_live, False)
    near_theirs = jnp.where(switches[0] > 0, near_theirs, -2.0)
    near_back = passed_along(near_theirs, "group", -1)
    leading = jnp.maximum(leading, jnp.where(switches[0] > 0, near_mine, -2.0))
    leading = jnp.maximum(leading, near_back)
    far_rows, far_live = passed_along((members, present), "group", half_way)
    far_mine, far_theirs = pair_maxima(members, present, far_rows, far_live, False)
    far_theirs = jnp.where(switches[1] > 0, far_theirs, -2.0)
    far_back = passed_along(far_theirs, "group", -half_way)
    leading = jnp.maximum(leading, jnp.where(switches[1] > 0, far_mine, -2.0))
    leading = jnp.maximum(leading, far_back)
    returned = lax.all_to_all(
        leading.reshape(owner_count, capacity), "dev", split_axis=0, concat_axis=0, tiled=True
    )
    return returned[owners, slot_ids]


def solution(mesh):
    placed = (P(("group", "dev"), None), P(("group", "dev"), None), P(), P(None, ("group", "dev")))
    return jax.shard_map(
        on_device, mesh=mesh, in_specs=placed, out_specs=P(("group", "dev")), check_vma=False
    )
```

profile of v0, /device:TPU:1, one launch (start us, length us, event | category | flops | bytes accessed | tf_op | source)
XLA Modules:
  0.0 380.6 jit_solution(14841604044870921491)
XLA Ops:
  0.0 1.8 fusion.10
  1.8 0.7 reduce
  2.5 0.7 select_reduce_fusion.2
  3.3 2.0 reduce-window.6
  5.8 1.4 fusion.11
  7.4 83.5 %scatter_fusion.1 = bf16[32,56,768]{2,1,0:T(8,128)(2,1)S(1)} fusion(bf16[32,56,768]{2,1,0:T(8,128)(2,1)S(1)} %broadcast_in_dim.63, s32[896]{0:T(1024)S(1)} %get-tuple-element.16, bf16[896,768]{1,0:T(8,128)(2,1)} %fusion.11), kind=kCustom, calls=%fused_computation.2 | custom fusion | bytes 4135936 | tf_op jit(solution)/shard_map/scatter | solution.py:49
  90.8 43.9 %all_to_all.26 = bf16[32,56,768]{2,1,0:T(8,128)(2,1)} all-to-all(bf16[32,56,768]{2,1,0:T(8,128)(2,1)S(1)} %scatter_fusion.1), channel_id=1, replica_groups=mesh['group'=8,'dev'=32] {'dev'}, dimensions={0} | all-to-all | bytes 5505024 | tf_op jit(solution)/shard_map/all_to_all | solution.py:57
  134.8 1.6 collective-permute-start.1
  136.4 6.1 %collective-permute-start.4 = (bf16[1792,768]{1,0:T(8,128)(2,1)}, bf16[1792,768]{1,0:T(8,128)(2,1)}, u32[]{:S(2)}, u32[]{:S(2)}) collective-permute-start(bf16[1792,768]{1,0:T(8,128)(2,1)} %bitcast.4), channel_id=1, source_target_pairs={{0,128},{32,160},{64,192},{96,224},{128,0},{160,32},{192,64},{224,... | collective-permute-start | bytes 8257544 | tf_op jit(solution)/shard_map/ppermute | solution.py:10
  142.4 46.3 %scatter_fusion = bf16[32,56]{1,0:T(8,128)(2,1)S(1)} fusion(bf16[32,56]{1,0:T(8,128)(2,1)S(1)} %broadcast_in_dim.34, s32[896]{0:T(1024)S(1)} %get-tuple-element.16, bf16[896]{0:T(1024)(128)(2,1)S(1)} %broadcast.149), kind=kCustom, calls=%fused_computation.1 | custom fusion | bytes 12544 | tf_op jit(solution)/shard_map/scatter | solution.py:51
  189.4 4.2 %all-to-all-start = ((bf16[32,1,56]{2,1,0:T(2,128)(2,1)}), bf16[32,1,56]{2,1,0:T(2,128)(2,1)S(1)}, u32[]{:S(2)}, u32[]{:S(2)}) async-start(bf16[32,1,56]{2,1,0:T(2,128)(2,1)} %copy.9), calls=%async_computation | async-start | bytes 32768 | tf_op jit(solution)/shard_map/all_to_all | solution.py:58
  195.5 5.1 %all-to-all-done = bf16[32,1,56]{2,1,0:T(2,128)(2,1)S(1)} async-done(((bf16[32,1,56]{2,1,0:T(2,128)(2,1)}), bf16[32,1,56]{2,1,0:T(2,128)(2,1)S(1)}, u32[]{:S(2)}, u32[]{:S(2)}) %all-to-all-start) | async-done | bytes 3616 | tf_op jit(solution)/shard_map/all_to_all | solution.py:58
  200.8 1.0 collective-permute-start
  202.1 61.4 %collective-permute-done.3 = bf16[1792]{0:T(1024)(128)(2,1)S(1)} collective-permute-done((bf16[1792]{0:T(1024)(128)(2,1)S(1)}, bf16[1792]{0:T(1024)(128)(2,1)S(1)}, u32[]{:S(2)}, u32[]{:S(2)}) %collective-permute-start.3) | collective-permute-done | bytes 3616 | tf_op jit(solution)/shard_map/ppermute | solution.py:10
  263.5 1.9 fusion.22
  265.5 5.0 %select_reduce_fusion = f32[896]{0:T(1024)S(1)} fusion(bf16[896,768]{1,0:T(8,128)(2,1)S(1)} %bitcast.43, bf16[1792,768]{1,0:T(8,128)(2,1)} %bitcast.4, s32[896]{0:T(1024)S(1)} %iota_add_fusion, pred[1792]{0:T(1024)(128)(4,1)S(1)} %broadcast_compare_fusion.2, pred[896]{0:T(1024)(128)(4,1)S(1)} %gt.62), kind=kOutput, calls=%fused_computation.3 | convolution fusion | flops 2474277888 | bytes 4138624 | tf_op jit(solution)/shard_map/dot_general | solution.py:23
  270.5 4.5 %fusion.24 = f32[896,1792]{1,0:T(8,128)S(1)} fusion(bf16[896,768]{1,0:T(8,128)(2,1)S(1)} %bitcast.44, bf16[1792,768]{1,0:T(8,128)(2,1)} %collective-permute-done.1), kind=kOutput, calls=%fused_computation.61 | convolution fusion | flops 2466250752 | bytes 10551296 | tf_op jit(solution)/shard_map/dot_general | solution.py:23
  274.9 4.5 %fusion.26 = f32[896,1792]{1,0:T(8,128)S(1)} fusion(bf16[896,768]{1,0:T(8,128)(2,1)S(1)} %bitcast.45, bf16[1792,768]{1,0:T(8,128)(2,1)} %collective-permute-done.4), kind=kOutput, calls=%fused_computation.63 | convolution fusion | flops 2466250752 | bytes 10551296 | tf_op jit(solution)/shard_map/dot_general | solution.py:23
  279.4 6.4 %fusion.25 = f32[896,1792]{1,0:T(8,128)} fusion(bf16[896,768]{1,0:T(8,128)(2,1)S(1)} %bitcast.40, bf16[1792,768]{1,0:T(8,128)(2,1)} %collective-permute-done.4), kind=kOutput, calls=%fused_computation.62 | convolution fusion | flops 2466250752 | bytes 10551296 | tf_op jit(solution)/shard_map/dot_general | solution.py:23
  285.8 10.6 %fusion.3 = (f32[896]{0:T(1024)S(1)}, f32[1792]{0:T(1024)S(1)}, f32[1792]{0:T(1024)S(1)}, f32[896]{0:T(1024)S(1)}, f32[896]{0:T(1024)S(1)}, /*index=5*/f32[1792]{0:T(1024)S(1)}, f32[1792]{0:T(1024)S(1)}, f32[896]{0:T(1024)S(1)}) fusion(pred[1792]{0:T(1024)(128)(4,1)S(1)} %broadcast_compare_fusion.1, pred[896]{0:T(1024)(128)(4,1)S(1)} %gt.59, ...), kind=kOutput, calls=%fused_computation.14 | convolution fusion | flops 2491929600 | bytes 23444736 | tf_op jit(solution)/shard_map/dot_general | solution.py:23
  296.5 59.4 %collective-permute-start.5 = (f32[1792]{0:T(1024)S(1)}, f32[1792]{0:T(1024)S(1)}, u32[]{:S(2)}, u32[]{:S(2)}) collective-permute-start(f32[1792]{0:T(1024)S(1)} %maximum_select_fusion.2), channel_id=1, source_target_pairs={{0,128},{32,160},{64,192},{96,224},{128,0},{160,32},{192,64},{224,... | collective-permute-start | bytes 21512 | tf_op jit(solution)/shard_map/ppermute | solution.py:10
  355.9 4.7 %select_reduce_fusion.1 = f32[896]{0:T(1024)S(1)} fusion(bf16[896,768]{1,0:T(8,128)(2,1)S(1)} %bitcast.42, bf16[1792,768]{1,0:T(8,128)(2,1)} %bitcast.4, pred[1792]{0:T(1024)(128)(4,1)S(1)} %broadcast_compare_fusion.2, pred[896]{0:T(1024)(128)(4,1)S(1)} %gt.59), kind=kOutput, calls=%fused_computation.5 | convolution fusion | flops 2474277888 | bytes 4135040 | tf_op jit(solution)/shard_map/dot_general | solution.py:23
  360.7 11.7 %all_to_all.27 = f32[32,1,56]{2,1,0:T(1,128)S(1)} all-to-all(f32[32,1,56]{2,1,0:T(1,128)S(1)} %all_to_all.20), channel_id=1, replica_groups=mesh['group'=8,'dev'=32] {'dev'}, dimensions={0} | all-to-all | bytes 14336 | tf_op jit(solution)/shard_map/all_to_all | solution.py:75
  372.4 8.2 %gather_fusion = f32[896]{0:T(1024)} fusion(f32[32,56]{1,0:T(8,128)S(1)} %bitcast.38, s32[896]{0:T(1024)S(1)} %get-tuple-element.15), kind=kCustom, calls=%fused_computation | custom fusion | bytes 14336 | tf_op jit(solution)/shard_map/gather | solution.py:78
  (36 shorter events, 2.5 us)
Async XLA Ops:
  0.0 5.8 %copy-start = (bf16[896,768]{1,0:T(8,128)(2,1)S(1)}, bf16[896,768]{1,0:T(8,128)(2,1)}, u32[]{:S(2)}) copy-start(bf16[896,768]{1,0:T(8,128)(2,1)} %param.4) | copy-start | bytes 4128772
  134.8 58.9 %copy-start.1 = (s32[2,1]{0,1:T(1,128)S(1)}, s32[2,1]{0,1:T(1,128)}, u32[]{:S(2)}) copy-start(s32[2,1]{0,1:T(1,128)} %param.7) | copy-start | bytes 28
  134.8 135.7 %collective-permute-start.1 = (bf16[1792,768]{1,0:T(8,128)(2,1)}, bf16[1792,768]{1,0:T(8,128)(2,1)}, u32[]{:S(2)}, u32[]{:S(2)}) collective-permute-start(bf16[1792,768]{1,0:T(8,128)(2,1)} %bitcast.4), channel_id=1, source_target_pairs={{0,32},{32,64},{64,96},{96,128},{128,160},{160,192},{192,224},{224... | collective-permute-start | bytes 8257544 | tf_op jit(solution)/shard_map/ppermute | solution.py:10
  136.4 138.6 %collective-permute-start.4 = (bf16[1792,768]{1,0:T(8,128)(2,1)}, bf16[1792,768]{1,0:T(8,128)(2,1)}, u32[]{:S(2)}, u32[]{:S(2)}) collective-permute-start(bf16[1792,768]{1,0:T(8,128)(2,1)} %bitcast.4), channel_id=1, source_target_pairs={{0,128},{32,160},{64,192},{96,224},{128,0},{160,32},{192,64},{224,... | collective-permute-start | bytes 8257544 | tf_op jit(solution)/shard_map/ppermute | solution.py:10
  189.4 11.2 %all-to-all-start = ((bf16[32,1,56]{2,1,0:T(2,128)(2,1)}), bf16[32,1,56]{2,1,0:T(2,128)(2,1)S(1)}, u32[]{:S(2)}, u32[]{:S(2)}) async-start(bf16[32,1,56]{2,1,0:T(2,128)(2,1)} %copy.9), calls=%async_computation | async-start | bytes 32768 | tf_op jit(solution)/shard_map/all_to_all | solution.py:58
  200.7 62.8 %collective-permute-start.3 = (bf16[1792]{0:T(1024)(128)(2,1)S(1)}, bf16[1792]{0:T(1024)(128)(2,1)S(1)}, u32[]{:S(2)}, u32[]{:S(2)}) collective-permute-start(bf16[1792]{0:T(1024)(128)(2,1)S(1)} %broadcast_in_dim_reshape.3), channel_id=1, source_target_pairs={{0,128},{32,160},{64,192},{96,224},{128,0},{160,32},{192,64},{224,... | collective-permute-start | bytes 10760 | tf_op jit(solution)/shard_map/ppermute | solution.py:10
  200.8 62.7 %collective-permute-start = (bf16[1792]{0:T(1024)(128)(2,1)S(1)}, bf16[1792]{0:T(1024)(128)(2,1)S(1)}, u32[]{:S(2)}, u32[]{:S(2)}) collective-permute-start(bf16[1792]{0:T(1024)(128)(2,1)S(1)} %broadcast_in_dim_reshape.3), channel_id=1, source_target_pairs={{0,32},{32,64},{64,96},{96,128},{128,160},{160,192},{192,224},{224... | collective-permute-start | bytes 10760 | tf_op jit(solution)/shard_map/ppermute | solution.py:10
  296.5 64.1 %collective-permute-start.5 = (f32[1792]{0:T(1024)S(1)}, f32[1792]{0:T(1024)S(1)}, u32[]{:S(2)}, u32[]{:S(2)}) collective-permute-start(f32[1792]{0:T(1024)S(1)} %maximum_select_fusion.2), channel_id=1, source_target_pairs={{0,128},{32,160},{64,192},{96,224},{128,0},{160,32},{192,64},{224,... | collective-permute-start | bytes 21512 | tf_op jit(solution)/shard_map/ppermute | solution.py:10
  355.9 4.7 %collective-permute-start.2 = (f32[1792]{0:T(1024)S(1)}, f32[1792]{0:T(1024)S(1)}, u32[]{:S(2)}, u32[]{:S(2)}) collective-permute-start(f32[1792]{0:T(1024)S(1)} %maximum_select_fusion.3), channel_id=1, source_target_pairs={{0,224},{32,0},{64,32},{96,64},{128,96},{160,128},{192,160},{224,1... | collective-permute-start | bytes 21512 | tf_op jit(solution)/shard_map/ppermute | solution.py:10
where the time goes:
time: 385 us; the launch traced here: 381 us
  local copies, waits for them, and re-layouts  142 us (37%)
  starting transfers between devices  72.4 us (19%)
  waiting for transfers between devices  66.5 us (17%)
  blocking collectives  55.6 us (14%)
  matrix products  35.7 us (9%)
  other arithmetic  7.01 us (2%)
    scatter x1, local copies, waits for them, and re-layouts, on_device(): jnp.zeros((owner_count, capacity, width), jnp.bfloat16).at[owners, slot_ids]  83.5 us
    ppermute x6, starting transfers between devices, passed_along(): return lax.ppermute(value, axis, pairs)  68.2 us
    ppermute x6, waiting for transfers between devices, passed_along(): return lax.ppermute(value, axis, pairs)  61.4 us
    scatter x1, local copies, waits for them, and re-layouts, on_device(): jnp.zeros((owner_count, capacity), jnp.bfloat16).at[owners, slot_ids]  46.3 us
    all_to_all x1, blocking collectives, on_device(): lax.all_to_all(outbox, 'dev', split_axis=0, concat_axis=0, tiled=True)  43.9 us
    dot_general x6, matrix products, pair_maxima(): lax.dot_general(top_rows, right_rows, (((1,), (1,)), ((), ())), preferred...  35.7 us
    all_to_all x1, blocking collectives, on_device(): lax.all_to_all(leading.reshape(owner_count, capacity), 'dev', split_axis=...  11.7 us
    gather x1, local copies, waits for them, and re-layouts, on_device(): return returned[owners, slot_ids]  8.2 us
  transfers between devices with their start and end apart: 7, of which 2 were waited for; matrix products, arithmetic and copies ran while one was open for 17% of the time, Pallas kernels for 0%

commit v1 on v0

v1 whole, which is shorter than its diff:
```python
import functools

import jax
import jax.numpy as jnp
from jax import lax
from jax.experimental import pallas as pl
from jax.experimental.pallas import tpu as pltpu
from jax.sharding import PartitionSpec as P

MESH = pl.DeviceIdType.MESH
SIDE = 4
CHIPS = SIDE * SIDE
OFFSETS = (
    (0, 0), (1, 0), (0, 1), (3, 0), (0, 3), (1, 1), (3, 3), (1, 3),
    (3, 1), (2, 0), (0, 2), (2, 2), (1, 2), (2, 1), (3, 2), (2, 3),
)
MARK = 4.0
DEAD = -8.0
COLS = 256


def kernel(cap, emb_ref, assign_ref, owner_of_ref, pair_ref, out_ref,
           unit, pack, sib_out, sib_in, outbox, members, near, far,
           best, partial, back_out, back_in, flags, flags_in, ret_out, ret_in,
           sib_sem, a2a_ss, a2a_rs, near_ss, near_rs, far_ss, far_rs,
           back_ss, back_rs, flag_ss, flag_rs, ret_ss, ret_rs):
    rows, width = emb_ref.shape
    chunk = 2 * cap
    total = CHIPS * chunk
    group = lax.axis_index("group")
    dev = lax.axis_index("dev")
    groups = lax.axis_size("group")
    core = lax.rem(dev, 2)
    y = lax.rem(dev // 2, SIDE)
    x = dev // (2 * SIDE)

    def chip_dev(off, sign, to_core):
        cx = lax.rem(x + sign * off[0] + SIDE, SIDE)
        cy = lax.rem(y + sign * off[1] + SIDE, SIDE)
        return (cx * SIDE + cy) * 2 + to_core

    def at_group(shift):
        return (lax.rem(group + shift + groups, groups), dev)

    other = 1 - core
    step = 1 - 2 * core
    half_way = groups // 2
    low = (group == 0) | (group == 2) | (group == 5) | (group == 7)
    sends_far = low == (core == 0)
    takes_far = low == (core == 1)

    barrier = pltpu.get_barrier_semaphore()
    for i, off in enumerate(OFFSETS):
        if i:
            pl.semaphore_signal(barrier, inc=1, device_id=(group, chip_dev(off, 1, core)), device_id_type=MESH)
        pl.semaphore_signal(barrier, inc=1, device_id=(group, chip_dev(off, 1, other)), device_id_type=MESH)
    for shift in (1, -1, half_way):
        pl.semaphore_signal(barrier, inc=1, device_id=at_group(shift), device_id_type=MESH)

    values = emb_ref[...].astype(jnp.float32)
    unit[...] = (values * lax.rsqrt(jnp.sum(values * values, axis=1, keepdims=True) + 1e-06)).astype(jnp.bfloat16)

    assign = assign_ref[...]
    ids = lax.broadcasted_iota(jnp.int32, (32, rows), 0)
    owner = jnp.sum(jnp.where(assign == ids, owner_of_ref[...], 0), axis=0, keepdims=True)
    mine = (owner == ids).astype(jnp.float32)
    before = (lax.broadcasted_iota(jnp.int32, (rows, rows), 0)
              < lax.broadcasted_iota(jnp.int32, (rows, rows), 1)).astype(jnp.float32).astype(jnp.bfloat16)
    counted = jnp.dot(mine.astype(jnp.bfloat16), before, preferred_element_type=jnp.float32)
    slot = jnp.sum(counted * mine, axis=0, keepdims=True).astype(jnp.int32)

    def places(to_core):
        place = jnp.full((1, rows), -1, jnp.int32)
        for i, off in enumerate(OFFSETS):
            place = jnp.where(owner == chip_dev(off, 1, to_core), i * cap + slot, place)
        return place

    def packed(place):
        hits = (place == lax.broadcasted_iota(jnp.int32, (CHIPS * cap, rows), 0)).astype(jnp.float32)
        live = jnp.sum(hits, axis=1, keepdims=True)
        got = jnp.dot(hits.astype(jnp.bfloat16), unit[...], preferred_element_type=jnp.float32)
        lane = lax.broadcasted_iota(jnp.int32, (CHIPS * cap, width), 1)
        return jnp.where((lane == 0) & (live < 0.5), MARK, got)

    place_same = places(core)
    place_other = places(other)
    sib_out[...] = packed(place_other).astype(jnp.bfloat16)

    pl.semaphore_wait(barrier, 2 * CHIPS - 1 + 3)

    sib = pltpu.make_async_remote_copy(
        src_ref=sib_out, dst_ref=sib_in, send_sem=sib_sem.at[0], recv_sem=sib_sem.at[1],
        device_id=(group, chip_dev((0, 0), 1, other)), device_id_type=MESH)
    sib.start()
    on = pair_ref[...].astype(jnp.float32)
    flags[...] = jnp.where(lax.broadcasted_iota(jnp.int32, (8, 128), 0) == 0, on[0:1, 0:1], on[1:2, 0:1])
    flag_copies = []
    for n, shift in enumerate((-1, half_way)):
        copy = pltpu.make_async_remote_copy(
            src_ref=flags, dst_ref=flags_in.at[n], send_sem=flag_ss.at[n], recv_sem=flag_rs.at[n],
            device_id=at_group(shift), device_id_type=MESH)
        copy.start()
        flag_copies.append(copy)

    pack[...] = packed(place_same)
    sib.wait()

    def chunk_of(i):
        top = pack[i * cap:(i + 1) * cap, :]
        return top

    from_sib = sib_in[...].astype(jnp.float32)
    sends = []
    for i, off in enumerate(OFFSETS):
        both = jnp.concatenate([chunk_of(i), from_sib[i * cap:(i + 1) * cap, :]], axis=0).astype(jnp.bfloat16)
        if i == 0:
            members[0:chunk, :] = both
            continue
        here = pl.ds(i * chunk, chunk)
        outbox[i * chunk:(i + 1) * chunk, :] = both
        copy = pltpu.make_async_remote_copy(
            src_ref=outbox.at[here], dst_ref=members.at[here], send_sem=a2a_ss.at[i], recv_sem=a2a_rs.at[i],
            device_id=(group, chip_dev(off, 1, core)), device_id_type=MESH)
        copy.start()
        sends.append(copy)

    def near_copy(i):
        here = pl.ds(i * chunk, chunk)
        return pltpu.make_async_remote_copy(
            src_ref=members.at[here], dst_ref=near.at[here], send_sem=near_ss.at[i], recv_sem=near_rs.at[i],
            device_id=at_group(step), device_id_type=MESH)

    def far_copy(i):
        here = pl.ds(i * chunk, chunk)
        return pltpu.make_async_remote_copy(
            src_ref=members.at[here], dst_ref=far.at[here], send_sem=far_ss.at[i], recv_sem=far_rs.at[i],
            device_id=at_group(half_way), device_id_type=MESH)

    for i in range(CHIPS):
        if i:
            sends[i - 1].wait_recv()
        near_copy(i).start()

        @pl.when(sends_far)
        def _(i=i):
            far_copy(i).start()

    tiles = 4
    height = total // tiles
    per_tile = CHIPS // tiles
    first_lane = (lax.broadcasted_iota(jnp.int32, (8, 128), 1) == 0).astype(jnp.float32).astype(jnp.bfloat16)
    marks = lax.dot_general(first_lane, members[:, 0:128], (((1,), (1,)), ((), ())), preferred_element_type=jnp.float32)
    col_bias = jnp.where(marks[0:1, :] > 2.0, DEAD, 0.0)

    def product(block, t, self_block, column_best):
        left_at = pl.ds(pl.multiple_of(t * height, height), height)
        left = block[left_at, :]
        row_bias = jnp.where(block[left_at, 0:128].astype(jnp.float32)[:, 0:1] > 2.0, DEAD, 0.0)
        row_bias = jnp.broadcast_to(row_bias, (height, COLS))
        lane_best = None
        for n in range(total // COLS):
            cols = slice(n * COLS, (n + 1) * COLS)
            sim = lax.dot_general(left, members[cols, :], (((1,), (1,)), ((), ())), preferred_element_type=jnp.float32)
            down = sim + row_bias
            if self_block:
                row_id = t * height + lax.broadcasted_iota(jnp.int32, (height, COLS), 0)
                col_id = n * COLS + lax.broadcasted_iota(jnp.int32, (height, COLS), 1)
                down = jnp.where(row_id == col_id, DEAD, down)
            else:
                across = sim + col_bias[:, cols]
                across = jnp.maximum(across[:, 0:128], across[:, 128:256])
                lane_best = across if lane_best is None else jnp.maximum(lane_best, across)
            down = jnp.max(down.reshape(height // 8, 8, COLS), axis=0)
            column_best[:, cols] = jnp.maximum(column_best[:, cols], down)
        if not self_block:
            partial[left_at, :] = lane_best

    def fold(into):
        for b in range(total // 128):
            lanes = slice(b * 128, (b + 1) * 128)
            into[:, lanes] = jnp.max(partial[lanes, :].T, axis=0, keepdims=True)

    best[...] = jnp.full(best.shape, DEAD, jnp.float32)

    def own_tile(t, carry):
        product(members, t, True, best.at[0])
        return carry

    lax.fori_loop(0, tiles, own_tile, 0)

    for copy in flag_copies:
        copy.wait()
    near_on = jnp.where(core == 0, flags[0:1, 0:1], flags_in[0, 0:1, 0:1])
    far_on = jnp.maximum(flags[1:2, 0:1], flags_in[1, 1:2, 0:1])

    def near_tile(t, carry):
        def wait(i, c):
            near_copy(i).wait_recv()
            return c

        lax.fori_loop(t * per_tile, (t + 1) * per_tile, wait, 0)
        product(near, t, False, best.at[1])
        return carry

    lax.fori_loop(0, tiles, near_tile, 0)
    fold(back_out.at[0])
    back_out[0] = jnp.where(near_on > 0.5, back_out[0], -2.0)
    near_back = pltpu.make_async_remote_copy(
        src_ref=back_out.at[0], dst_ref=back_in.at[0], send_sem=back_ss.at[0], recv_sem=back_rs.at[0],
        device_id=at_group(-step), device_id_type=MESH)
    near_back.start()
    far_back = pltpu.make_async_remote_copy(
        src_ref=back_out.at[1], dst_ref=back_in.at[1], send_sem=back_ss.at[1], recv_sem=back_rs.at[1],
        device_id=at_group(half_way), device_id_type=MESH)

    @pl.when(takes_far)
    def _():
        def far_tile(t, carry):
            def wait(i, c):
                far_copy(i).wait_recv()
                return c

            lax.fori_loop(t * per_tile, (t + 1) * per_tile, wait, 0)
            product(far, t, False, best.at[2])
            return carry

        lax.fori_loop(0, tiles, far_tile, 0)
        fold(back_out.at[1])
        back_out[1] = jnp.where(far_on > 0.5, back_out[1], -2.0)
        far_back.start()
        back_in[1] = jnp.full((1, total), -2.0, jnp.float32)

    near_back.wait_recv()

    @pl.when(sends_far)
    def _():
        far_back.wait_recv()

    leading = jnp.maximum(jnp.max(best[0], axis=0, keepdims=True), -1.0)
    leading = jnp.maximum(leading, jnp.where(near_on > 0.5, jnp.max(best[1], axis=0, keepdims=True), -2.0))
    leading = jnp.maximum(leading, jnp.where(far_on > 0.5, jnp.max(best[2], axis=0, keepdims=True), -2.0))
    leading = jnp.maximum(leading, jnp.maximum(back_in[0], back_in[1]))

    returns = []
    ret_out[...] = jnp.zeros(ret_out.shape, jnp.float32)
    for i, off in enumerate(OFFSETS):
        for q, to_core in enumerate((core, other)):
            j = 2 * i + q
            ret_out[j, 0:1, 0:cap] = leading[:, j * cap:(j + 1) * cap]
            if j == 0:
                ret_in[0] = ret_out[0]
                continue
            copy = pltpu.make_async_remote_copy(
                src_ref=ret_out.at[j], dst_ref=ret_in.at[j], send_sem=ret_ss.at[j], recv_sem=ret_rs.at[j],
                device_id=(group, chip_dev(off, -1, to_core)), device_id_type=MESH)
            copy.start()
            returns.append(copy)

    index = jnp.full((1, rows), -1, jnp.int32)
    for i, off in enumerate(OFFSETS):
        for q, to_core in enumerate((core, other)):
            index = jnp.where(owner == chip_dev(off, 1, to_core), 2 * i + q, index)
    chosen = (index == ids).astype(jnp.float32).astype(jnp.bfloat16)
    for copy in returns:
        copy.wait_recv()
    got = ret_in[:, 0, :]
    spread = jnp.zeros((128, rows), jnp.float32)
    for _ in range(3):
        part = got.astype(jnp.bfloat16)
        got = got - part.astype(jnp.float32)
        spread = spread + lax.dot_general(part, chosen, (((0,), (0,)), ((), ())), preferred_element_type=jnp.float32)
    pick = lax.broadcasted_iota(jnp.int32, (128, rows), 0) == slot
    out_ref[...] = jnp.sum(jnp.where(pick, spread, 0.0), axis=0, keepdims=True)

    for copy in sends + returns + [near_back]:
        copy.wait_send()
    for i in range(CHIPS):
        near_copy(i).wait_send()

    @pl.when(sends_far)
    def _():
        for i in range(CHIPS):
            far_copy(i).wait_send()

    @pl.when(takes_far)
    def _():
        far_back.wait_send()


def on_device(embeddings, assignment, owner_of, pair_on):
    rows, width = embeddings.shape
    owners = owner_of.shape[0]
    cap = 2 * rows // owners
    total = owners * cap
    half = total // 2
    bf16, f32 = jnp.bfloat16, jnp.float32
    dma = pltpu.SemaphoreType.DMA
    out = pl.pallas_call(
        functools.partial(kernel, cap),
        out_shape=jax.ShapeDtypeStruct((1, rows), f32),
        in_specs=[pl.BlockSpec(memory_space=pltpu.VMEM)] * 4,
        out_specs=pl.BlockSpec(memory_space=pltpu.VMEM),
        scratch_shapes=[
            pltpu.VMEM((rows, width), bf16),
            pltpu.VMEM((half, width), f32),
            pltpu.VMEM((half, width), bf16),
            pltpu.VMEM((half, width), bf16),
            pltpu.VMEM((total, width), bf16),
            pltpu.VMEM((total, width), bf16),
            pltpu.VMEM((total, width), bf16),
            pltpu.VMEM((total, width), bf16),
            pltpu.VMEM((3, 8, total), f32),
            pltpu.VMEM((total, 128), f32),
            pltpu.VMEM((2, 1, total), f32),
            pltpu.VMEM((2, 1, total), f32),
            pltpu.VMEM((8, 128), f32),
            pltpu.VMEM((2, 8, 128), f32),
            pltpu.VMEM((owners, 1, 128), f32),
            pltpu.VMEM((owners, 1, 128), f32),
            dma((2,)),
            dma((CHIPS,)), dma((CHIPS,)),
            dma((CHIPS,)), dma((CHIPS,)),
            dma((CHIPS,)), dma((CHIPS,)),
            dma((2,)), dma((2,)),
            dma((2,)), dma((2,)),
            dma((owners,)), dma((owners,)),
        ],
        compiler_params=pltpu.CompilerParams(
            collective_id=0, has_side_effects=True, vmem_limit_bytes=56 * 2**20),
        cost_estimate=pl.CostEstimate(flops=6 * total * total * width, bytes_accessed=2 * rows * width, transcendentals=0),
        name="semdedup",
    )(embeddings, assignment.reshape(1, rows), owner_of.reshape(owners, 1), pair_on)
    return out.reshape(rows)


def solution(mesh):
    placed = (P(("group", "dev"), None), P(("group", "dev"), None), P(), P(None, ("group", "dev")))
    return jax.shard_map(
        on_device, mesh=mesh, in_specs=placed, out_specs=P(("group", "dev")), check_vma=False
    )
```

time: 385 us -> 135 us (0.35); the launches traced: 381 us -> 135 us
  local copies, waits for them, and re-layouts: 142 us -> 2.62 us
  Pallas kernels: 0 us -> 131 us
  starting transfers between devices: 72.4 us -> 0 us
  waiting for transfers between devices: 66.5 us -> 0 us
  blocking collectives: 55.6 us -> 0 us
  matrix products: 35.7 us -> 0 us
  other arithmetic: 7.01 us -> 1.28 us
    pallas_call x0 -> x1, Pallas kernels: none -> 131 us  [on_device(): pl.pallas_call(functools.partial(kernel, cap), out_shape=jax.ShapeDtypeSt...]
    scatter x2 -> x0, local copies, waits for them, and re-layouts: 130 us -> none  [the longest x1 83.5 us: on_device(): jnp.zeros((owner_count, capacity, width), jnp.bfloat16).at[owners, slot_ids]]
    ppermute x6 -> x0, starting transfers between devices: 68.2 us -> none  [passed_along(): return lax.ppermute(value, axis, pairs)]
    ppermute x6 -> x0, waiting for transfers between devices: 61.4 us -> none  [passed_along(): return lax.ppermute(value, axis, pairs)]
    all_to_all x2 -> x0, blocking collectives: 55.6 us -> none  [the longest x1 43.9 us: on_device(): lax.all_to_all(outbox, 'dev', split_axis=0, concat_axis=0, tiled=True)]
    dot_general x6 -> x0, matrix products: 35.7 us -> none  [pair_maxima(): lax.dot_general(top_rows, right_rows, (((1,), (1,)), ((), ())), preferred...]
    gather x1 -> x0, local copies, waits for them, and re-layouts: 8.2 us -> none  [on_device(): return returned[owners, slot_ids]]
    all_to_all x1 -> x0, waiting for transfers between devices: 5.11 us -> none  [on_device(): lax.all_to_all(slot_marks, 'dev', split_axis=0, concat_axis=0, tiled=True)]
  transfers between devices with their start and end apart: 7 -> 0, of which waited for: 2 -> 0; matrix products, arithmetic and copies ran while one was open for 17% -> 0% of each run, Pallas kernels for 0% -> 0%
where the time goes in v1:
time: 135 us
  Pallas kernels  131 us (97%)
  local copies, waits for them, and re-layouts  2.62 us (2%)
    pallas_call x1, Pallas kernels, on_device(): pl.pallas_call(functools.partial(kernel, cap), out_shape=jax.ShapeDtypeSt...  131 us

profile of v1, /device:TPU:1, one launch (start us, length us, event | category | flops | bytes accessed | tf_op | source)
XLA Modules:
  0.0 134.9 jit_solution(18277550783836836319)
XLA Ops:
  0.0 1.3 copy.6.pair_ref
  1.3 1.3 copy.5.owner_of_ref
  2.6 130.9 %semdedup.1 = f32[1,896]{1,0:T(1,128)} custom-call(bf16[896,768]{1,0:T(8,128)(2,1)} %emb_ref.1, s32[1,896]{1,0:T(1,128)} %bitcast.3, s32[32,1]{1,0:T(8,128)} %copy.5.owner_of_ref, s32[2,1]{1,0:T(2,128)} %copy.6.pair_ref), custom_call_target="tpu_custom_call" | custom-call | flops 14797504512 | bytes 1376256 | tf_op jit(solution)/shard_map/semdedup/pallas_call | solution.py:298
  133.6 1.3 reduce

commit v2 on v1

v2 whole, which is shorter than its diff:
```python
import functools

import jax
import jax.numpy as jnp
from jax import lax
from jax.experimental import pallas as pl
from jax.experimental.pallas import tpu as pltpu
from jax.sharding import PartitionSpec as P

MESH = pl.DeviceIdType.MESH
SIDE = 4
CHIPS = SIDE * SIDE
OFFSETS = (
    (0, 0), (1, 0), (0, 1), (3, 0), (0, 3), (1, 1), (3, 3), (1, 3),
    (3, 1), (2, 0), (0, 2), (2, 2), (1, 2), (2, 1), (3, 2), (2, 3),
)
MARK = 4.0
DEAD = -8.0
COLS = 256
PIECES = 4
AT_ONCE = (15, 7)


def kernel(cap, emb_ref, assign_ref, owner_of_ref, pair_ref, out_ref,
           unit, pack, hits_other, hits_same, sib_out, sib_in, outbox, members, near, far,
           code, relayed, unit_in, code_in,
           best, partial, back_out, back_in, flags, flags_in, ret_out, ret_in,
           sib_ss, sib_rs, a2a_ss, a2a_rs, near_ss, near_rs, raw_ss, raw_rs, hop_ss, hop_rs, code_sem,
           back_sem, flag_ss, flag_rs, ret_ss, ret_rs):
    rows, width = emb_ref.shape
    chunk = 2 * cap
    total = CHIPS * chunk
    group = lax.axis_index("group")
    dev = lax.axis_index("dev")
    groups = lax.axis_size("group")
    core = lax.rem(dev, 2)
    y = lax.rem(dev // 2, SIDE)
    x = dev // (2 * SIDE)

    def chip_dev(off, sign, to_core):
        cx = lax.rem(x + sign * off[0] + SIDE, SIDE)
        cy = lax.rem(y + sign * off[1] + SIDE, SIDE)
        return (cx * SIDE + cy) * 2 + to_core

    def at_group(shift):
        return (lax.rem(group + shift + groups, groups), dev)

    other = 1 - core
    step = 1 - 2 * core
    half_way = groups // 2

    def any_of(*numbers):
        hit = group == numbers[0]
        for number in numbers[1:]:
            hit = hit | (group == number)
        return hit

    sends_far = any_of(0, 2, 5, 7)
    takes_far = any_of(1, 3, 4, 6)
    relays = (any_of(0, 2, 3, 5), any_of(2, 4, 5, 7))

    barrier = pltpu.get_barrier_semaphore()
    for i, off in enumerate(OFFSETS):
        if i:
            pl.semaphore_signal(barrier, inc=1, device_id=(group, chip_dev(off, 1, core)), device_id_type=MESH)
        pl.semaphore_signal(barrier, inc=1, device_id=(group, chip_dev(off, 1, other)), device_id_type=MESH)
    far_group = lax.rem(group + half_way, groups)
    for i, off in enumerate(OFFSETS):
        for to_core in (core, other):
            pl.semaphore_signal(barrier, inc=1, device_id=(far_group, chip_dev(off, 1, to_core)), device_id_type=MESH)
    shifts = (1, -1, 3, -3)
    for shift in shifts:
        pl.semaphore_signal(barrier, inc=1, device_id=at_group(shift), device_id_type=MESH)

    values = emb_ref[...].astype(jnp.float32)
    unit[...] = (values * lax.rsqrt(jnp.sum(values * values, axis=1, keepdims=True) + 1e-06)).astype(jnp.bfloat16)

    assign = assign_ref[...]
    ids = lax.broadcasted_iota(jnp.int32, (32, rows), 0)
    owner = jnp.zeros((1, rows), jnp.int32)
    for n in range(owner_of_ref.shape[0]):
        owner = jnp.where(assign == n, owner_of_ref[n], owner)
    mine = (owner == ids).astype(jnp.float32)
    before = (lax.broadcasted_iota(jnp.int32, (rows, rows), 0)
              < lax.broadcasted_iota(jnp.int32, (rows, rows), 1)).astype(jnp.float32).astype(jnp.bfloat16)
    counted = jnp.dot(mine.astype(jnp.bfloat16), before, preferred_element_type=jnp.float32)
    slot = jnp.sum(counted * mine, axis=0, keepdims=True).astype(jnp.int32)

    code[...] = (owner * 64 + slot).astype(jnp.float32)

    piece = rows // (2 * PIECES)

    def raw_copy(way, k):
        return pltpu.make_async_remote_copy(
            src_ref=unit.at[pl.ds((way * PIECES + k) * piece, piece)], dst_ref=relayed.at[way, k],
            send_sem=raw_ss.at[way, k], recv_sem=raw_rs.at[way, k],
            device_id=at_group(-3 if way else 3), device_id_type=MESH)

    def hop_copy(way, k):
        return pltpu.make_async_remote_copy(
            src_ref=relayed.at[way, k], dst_ref=unit_in.at[pl.ds((way * PIECES + k) * piece, piece)],
            send_sem=hop_ss.at[way, k], recv_sem=hop_rs.at[way, k],
            device_id=at_group(-1 if way else 1), device_id_type=MESH)

    code_copy = pltpu.make_async_remote_copy(
        src_ref=code, dst_ref=code_in, send_sem=code_sem.at[0], recv_sem=code_sem.at[1],
        device_id=at_group(half_way), device_id_type=MESH)

    def places(owner, slot, to_core):
        place = jnp.full((1, rows), -1, jnp.int32)
        for i, off in enumerate(OFFSETS):
            place = jnp.where(owner == chip_dev(off, 1, to_core), i * cap + slot, place)
        return place

    def set_hits(into, owner, slot, to_core):
        place = places(owner, slot, to_core)
        into[...] = (place == lax.broadcasted_iota(jnp.int32, (CHIPS * cap, rows), 0)).astype(jnp.float32).astype(jnp.bfloat16)

    def packed(hits, source):
        live = jnp.sum(hits[...].astype(jnp.float32), axis=1, keepdims=True)
        got = jnp.dot(hits[...], source[...], preferred_element_type=jnp.float32)
        lane = lax.broadcasted_iota(jnp.int32, (CHIPS * cap, width), 1)
        return jnp.where((lane == 0) & (live < 0.5), MARK, got)

    def sib_copy(turn):
        return pltpu.make_async_remote_copy(
            src_ref=sib_out.at[turn], dst_ref=sib_in.at[turn], send_sem=sib_ss.at[turn], recv_sem=sib_rs.at[turn],
            device_id=(group, chip_dev((0, 0), 1, other)), device_id_type=MESH)

    def chunk_copy(turn, i):
        here = pl.ds(i * chunk, chunk)
        return pltpu.make_async_remote_copy(
            src_ref=outbox.at[turn, here], dst_ref=(members, far)[turn].at[here],
            send_sem=a2a_ss.at[turn, i], recv_sem=a2a_rs.at[turn, i],
            device_id=(group, chip_dev(OFFSETS[i], 1, core)), device_id_type=MESH)

    def pack_all(turn, source):
        sib_out[turn] = packed(hits_other, source).astype(jnp.bfloat16)
        sib_copy(turn).start()
        pack[...] = packed(hits_same, source)
        sib_copy(turn).wait()
        from_sib = sib_in[turn].astype(jnp.float32)
        for i in range(CHIPS):
            both = jnp.concatenate(
                [pack[i * cap:(i + 1) * cap, :], from_sib[i * cap:(i + 1) * cap, :]], axis=0).astype(jnp.bfloat16)
            if i == 0:
                (members, far)[turn][0:chunk, :] = both
                continue
            outbox[turn, i * chunk:(i + 1) * chunk, :] = both
            if i <= AT_ONCE[turn]:
                chunk_copy(turn, i).start()

    def send_rest(turn):
        for i in range(AT_ONCE[turn] + 1, CHIPS):
            chunk_copy(turn, i).start()

    set_hits(hits_other, owner, slot, other)
    pl.semaphore_wait(barrier, 4 * CHIPS - 1 + len(shifts))

    @pl.when(sends_far)
    def _():
        for k in range(PIECES):
            for way in range(2):
                raw_copy(way, k).start()
        code_copy.start()

    set_hits(hits_same, owner, slot, core)
    pack_all(0, unit)
    flags[...] = jnp.where(lax.broadcasted_iota(jnp.int32, (8, 128), 0) == 0, pair_ref[0, 0], pair_ref[0, 1]).astype(jnp.float32)
    flag_copies = []
    for n, shift in enumerate((-1, half_way)):
        copy = pltpu.make_async_remote_copy(
            src_ref=flags, dst_ref=flags_in.at[n], send_sem=flag_ss.at[n], recv_sem=flag_rs.at[n],
            device_id=at_group(shift), device_id_type=MESH)
        copy.start()
        flag_copies.append(copy)

    @pl.when(takes_far)
    def _():
        code_copy.wait_recv()
        whole = code_in[...].astype(jnp.int32)
        set_hits(hits_other, whole // 64, whole % 64, other)
        set_hits(hits_same, whole // 64, whole % 64, core)

    for k in range(PIECES):
        for way in range(2):
            @pl.when(relays[way])
            def _(way=way, k=k):
                raw_copy(way, k).wait_recv()
                hop_copy(way, k).start()

    def near_copy(i):
        here = pl.ds(i * chunk, chunk)
        return pltpu.make_async_remote_copy(
            src_ref=members.at[here], dst_ref=near.at[here], send_sem=near_ss.at[i], recv_sem=near_rs.at[i],
            device_id=at_group(step), device_id_type=MESH)

    for i in range(1, CHIPS):
        chunk_copy(0, i).wait_recv()
    for i in range(CHIPS):
        near_copy(i).start()

    @pl.when(takes_far)
    def _():
        for k in range(PIECES):
            for way in range(2):
                hop_copy(way, k).wait_recv()
        pack_all(1, unit_in)

    tiles = 4
    height = total // tiles
    per_tile = CHIPS // tiles
    first_lane = (lax.broadcasted_iota(jnp.int32, (8, 128), 1) == 0).astype(jnp.float32).astype(jnp.bfloat16)
    marks = lax.dot_general(first_lane, members[:, 0:128], (((1,), (1,)), ((), ())), preferred_element_type=jnp.float32)
    col_bias = jnp.where(marks[0:1, :] > 2.0, DEAD, 0.0)

    def product(block, t, self_block, column_best):
        left_at = pl.ds(t * height if isinstance(t, int) else pl.multiple_of(t * height, height), height)
        left = block[left_at, :]
        row_bias = jnp.where(block[left_at, 0:128].astype(jnp.float32)[:, 0:1] > 2.0, DEAD, 0.0)
        row_bias = jnp.broadcast_to(row_bias, (height, COLS))
        lane_best = None
        for n in range(total // COLS):
            cols = slice(n * COLS, (n + 1) * COLS)
            sim = lax.dot_general(left, members[cols, :], (((1,), (1,)), ((), ())), preferred_element_type=jnp.float32)
            down = sim + row_bias
            if self_block:
                row_id = t * height + lax.broadcasted_iota(jnp.int32, (height, COLS), 0)
                col_id = n * COLS + lax.broadcasted_iota(jnp.int32, (height, COLS), 1)
                down = jnp.where(row_id == col_id, DEAD, down)
            else:
                across = sim + col_bias[:, cols]
                across = jnp.maximum(across[:, 0:128], across[:, 128:256])
                lane_best = across if lane_best is None else jnp.maximum(lane_best, across)
            down = jnp.max(down.reshape(height // 8, 8, COLS), axis=0)
            column_best[:, cols] = jnp.maximum(column_best[:, cols], down)
        if not self_block:
            partial[left_at, :] = lane_best

    def fold(into):
        for b in range(total // 128):
            lanes = slice(b * 128, (b + 1) * 128)
            into[:, lanes] = jnp.max(partial[lanes, :].T, axis=0, keepdims=True)

    best[...] = jnp.full(best.shape, DEAD, jnp.float32)

    def own_tile(t, carry):
        product(members, t, True, best.at[0])
        return carry

    lax.fori_loop(0, tiles, own_tile, 0)

    @pl.when(takes_far)
    def _():
        send_rest(1)

    for copy in flag_copies:
        copy.wait()
    near_on = jnp.where(core == 0, flags[0:1, 0:1], flags_in[0, 0:1, 0:1])
    far_on = jnp.maximum(flags[1:2, 0:1], flags_in[1, 1:2, 0:1])

    def near_tile(t, carry):
        def wait(i, c):
            near_copy(i).wait_recv()
            return c

        lax.fori_loop(t * per_tile, (t + 1) * per_tile, wait, 0)
        product(near, t, False, best.at[1])
        return carry

    lax.fori_loop(0, tiles, near_tile, 0)
    fold(back_out.at[0])
    back_out[0] = jnp.where(near_on > 0.5, back_out[0], -2.0)
    near_back = pltpu.make_async_remote_copy(
        src_ref=back_out.at[0], dst_ref=back_in, send_sem=back_sem.at[0], recv_sem=back_sem.at[1],
        device_id=at_group(-step), device_id_type=MESH)
    near_back.start()

    def ret_copy(turn, j):
        off, to_core = OFFSETS[j // 2], (core, other)[j % 2]
        to_group = lax.rem(group + half_way, groups) if turn else group
        return pltpu.make_async_remote_copy(
            src_ref=ret_out.at[turn, j], dst_ref=ret_in.at[turn, j], send_sem=ret_ss.at[turn, j], recv_sem=ret_rs.at[turn, j],
            device_id=(to_group, chip_dev(off, -1, to_core)), device_id_type=MESH)

    ret_out[...] = jnp.zeros(ret_out.shape, jnp.float32)

    @pl.when(takes_far)
    def _():
        for t in range(tiles):
            for i in range(max(1, t * per_tile), (t + 1) * per_tile):
                chunk_copy(1, i).wait_recv()
            product(far, t, False, best.at[2])
        fold(back_out.at[1])
        theirs = jnp.where(far_on > 0.5, back_out[1], -2.0)
        for j in range(2 * CHIPS):
            ret_out[1, j, 0:1, 0:cap] = theirs[:, j * cap:(j + 1) * cap]
            ret_copy(1, j).start()
        ret_in[1] = jnp.full(ret_in.shape[1:], -2.0, jnp.float32)

    near_back.wait_recv()
    leading = jnp.maximum(jnp.max(best[0], axis=0, keepdims=True), -1.0)
    leading = jnp.maximum(leading, jnp.where(near_on > 0.5, jnp.max(best[1], axis=0, keepdims=True), -2.0))
    leading = jnp.maximum(leading, jnp.where(far_on > 0.5, jnp.max(best[2], axis=0, keepdims=True), -2.0))
    leading = jnp.maximum(leading, back_in[...])

    for j in range(2 * CHIPS):
        ret_out[0, j, 0:1, 0:cap] = leading[:, j * cap:(j + 1) * cap]
        if j:
            ret_copy(0, j).start()
    ret_in[0, 0] = ret_out[0, 0]

    index = jnp.full((1, rows), -1, jnp.int32)
    for i, off in enumerate(OFFSETS):
        for q, to_core in enumerate((core, other)):
            index = jnp.where(owner == chip_dev(off, 1, to_core), 2 * i + q, index)
    chosen = (index == ids).astype(jnp.float32).astype(jnp.bfloat16)
    for j in range(1, 2 * CHIPS):
        ret_copy(0, j).wait_recv()

    @pl.when(sends_far)
    def _():
        for j in range(2 * CHIPS):
            ret_copy(1, j).wait_recv()

    got = jnp.maximum(ret_in[0, :, 0, :], ret_in[1, :, 0, :])
    spread = jnp.zeros((128, rows), jnp.float32)
    for _ in range(3):
        part = got.astype(jnp.bfloat16)
        got = got - part.astype(jnp.float32)
        spread = spread + lax.dot_general(part, chosen, (((0,), (0,)), ((), ())), preferred_element_type=jnp.float32)
    pick = lax.broadcasted_iota(jnp.int32, (128, rows), 0) == slot
    out_ref[...] = jnp.sum(jnp.where(pick, spread, 0.0), axis=0, keepdims=True)

    near_back.wait_send()
    for j in range(1, 2 * CHIPS):
        ret_copy(0, j).wait_send()
    for i in range(CHIPS):
        near_copy(i).wait_send()
        if i:
            chunk_copy(0, i).wait_send()

    @pl.when(sends_far)
    def _():
        for k in range(PIECES):
            for way in range(2):
                raw_copy(way, k).wait_send()
        code_copy.wait_send()

    for way in range(2):
        @pl.when(relays[way])
        def _(way=way):
            for k in range(PIECES):
                hop_copy(way, k).wait_send()

    @pl.when(takes_far)
    def _():
        for i in range(1, CHIPS):
            chunk_copy(1, i).wait_send()
        for j in range(2 * CHIPS):
            ret_copy(1, j).wait_send()


def on_device(embeddings, assignment, owner_of, pair_on):
    rows, width = embeddings.shape
    owners = owner_of.shape[0]
    cap = 2 * rows // owners
    total = owners * cap
    half = total // 2
    bf16, f32 = jnp.bfloat16, jnp.float32
    dma = pltpu.SemaphoreType.DMA
    out = pl.pallas_call(
        functools.partial(kernel, cap),
        out_shape=jax.ShapeDtypeStruct((1, rows), f32),
        in_specs=[pl.BlockSpec(memory_space=pltpu.VMEM)] * 2 + [pl.BlockSpec(memory_space=pltpu.SMEM)] * 2,
        out_specs=pl.BlockSpec(memory_space=pltpu.VMEM),
        scratch_shapes=[
            pltpu.VMEM((rows, width), bf16),
            pltpu.VMEM((half, width), f32),
            pltpu.VMEM((half, rows), bf16),
            pltpu.VMEM((half, rows), bf16),
            pltpu.VMEM((2, half, width), bf16),
            pltpu.VMEM((2, half, width), bf16),
            pltpu.VMEM((2, total, width), bf16),
            pltpu.VMEM((total, width), bf16),
            pltpu.VMEM((total, width), bf16),
            pltpu.VMEM((total, width), bf16),
            pltpu.VMEM((1, rows), f32),
            pltpu.VMEM((2, PIECES, rows // (2 * PIECES), width), bf16),
            pltpu.VMEM((rows, width), bf16),
            pltpu.VMEM((1, rows), f32),
            pltpu.VMEM((3, 8, total), f32),
            pltpu.VMEM((total, 128), f32),
            pltpu.VMEM((2, 1, total), f32),
            pltpu.VMEM((1, total), f32),
            pltpu.VMEM((8, 128), f32),
            pltpu.VMEM((2, 8, 128), f32),
            pltpu.VMEM((2, owners, 1, 128), f32),
            pltpu.VMEM((2, owners, 1, 128), f32),
            dma((2,)), dma((2,)),
            dma((2, CHIPS)), dma((2, CHIPS)),
            dma((CHIPS,)), dma((CHIPS,)),
            dma((2, PIECES)), dma((2, PIECES)),
            dma((2, PIECES)), dma((2, PIECES)),
            dma((2,)),
            dma((2,)),
            dma((2,)), dma((2,)),
            dma((2, owners)), dma((2, owners)),
        ],
        compiler_params=pltpu.CompilerParams(
            collective_id=0, has_side_effects=True, vmem_limit_bytes=56 * 2**20),
        cost_estimate=pl.CostEstimate(flops=6 * total * total * width, bytes_accessed=2 * rows * width, transcendentals=0),
        name="semdedup",
    )(embeddings, assignment.reshape(1, rows), owner_of, pair_on.reshape(1, 2))
    return out.reshape(rows)


def solution(mesh):
    placed = (P(("group", "dev"), None), P(("group", "dev"), None), P(), P(None, ("group", "dev")))
    return jax.shard_map(
        on_device, mesh=mesh, in_specs=placed, out_specs=P(("group", "dev")), check_vma=False
    )
```

time: 135 us -> 121 us (0.90)
  Pallas kernels: 131 us -> 119 us
  local copies, waits for them, and re-layouts: 2.62 us -> 0 us
    pallas_call x1, Pallas kernels: 131 us -> 119 us  [on_device(): pl.pallas_call(functools.partial(kernel, cap), out_shape=jax.ShapeDtypeSt...]
where the time goes in v2:
time: 121 us; the launch traced here: 120 us
  Pallas kernels  119 us (98%)
  other arithmetic  1.29 us (1%)
    pallas_call x1, Pallas kernels, on_device(): pl.pallas_call(functools.partial(kernel, cap), out_shape=jax.ShapeDtypeSt...  119 us

profile of v2, /device:TPU:1, one launch (start us, length us, event | category | flops | bytes accessed | tf_op | source)
XLA Modules:
  0.0 120.1 jit_solution(8089994182286166412)
XLA Ops:
  0.0 118.8 %semdedup.1 = f32[1,896]{1,0:T(1,128)} custom-call(bf16[896,768]{1,0:T(8,128)(2,1)} %emb_ref.1, s32[1,896]{1,0:T(1,128)} %bitcast.2, s32[32]{0:T(128)} %owner_of_ref.1, s32[1,2]{1,0:T(1,128)} %bitcast.3), custom_call_target="tpu_custom_call" | custom-call | flops 14797504512 | bytes 1376256 | tf_op jit(solution)/shard_map/semdedup/pallas_call | solution.py:372
  118.8 1.3 %reduce = f32[896]{0:T(1024)} reduce(f32[1,896]{1,0:T(1,128)} %semdedup.1, f32[]{:T(128)} %constant.3), dimensions={0}, to_apply=%pallas_call.3.reduce_sub_computation | reduce | bytes 7172 | tf_op jit(solution)/shard_map/semdedup/pallas_call | solution.py:372

commit v3 on v2

v3 whole, which is shorter than its diff:
```python
import functools

import jax
import jax.numpy as jnp
from jax import lax
from jax.experimental import pallas as pl
from jax.experimental.pallas import tpu as pltpu
from jax.sharding import PartitionSpec as P

MESH = pl.DeviceIdType.MESH
SIDE = 4
CHIPS = SIDE * SIDE
OFFSETS = (
    (0, 0), (2, 2), (1, 2), (2, 1), (3, 2), (2, 3), (1, 1), (3, 3),
    (1, 3), (3, 1), (2, 0), (0, 2), (1, 0), (0, 1), (3, 0), (0, 3),
)
MARK = 4.0
DEAD = -8.0
COLS = 256
PIECES = 7
AHEAD = 7
NEAR_SENDER = (0, 0, 0, 0, 0, 0, 0)
NEAR_TAKER = (0, 0, 6, 9, 12, 16, 16)
PARTS = (((0, 4), (4, 8), (8, 12), (12, 16)), ((0, 2), (2, 4), (4, 6), (6, 8), (8, 12), (12, 16)))
EARLY = (2, 4, 6)


def kernel(cap, emb_ref, assign_ref, owner_of_ref, pair_ref, out_ref,
           unit, in_order, hits_other, hits_same, sib_out, sib_in, outbox, members, near, far,
           base_out, relayed, unit_in, base_in,
           best, partial, back_out, back_in, flags, flags_in, ret_out, ret_in,
           sib_ss, sib_rs, a2a_ss, a2a_rs, near_ss, near_rs, raw_ss, raw_rs, hop_ss, hop_rs, base_sem,
           back_sem, flag_ss, flag_rs, ret_ss, ret_rs):
    rows, width = emb_ref.shape
    chunk = 2 * cap
    total = CHIPS * chunk
    group = lax.axis_index("group")
    dev = lax.axis_index("dev")
    groups = lax.axis_size("group")
    core = lax.rem(dev, 2)
    y = lax.rem(dev // 2, SIDE)
    x = dev // (2 * SIDE)

    def chip_dev(off, sign, to_core):
        cx = lax.rem(x + sign * off[0] + SIDE, SIDE)
        cy = lax.rem(y + sign * off[1] + SIDE, SIDE)
        return (cx * SIDE + cy) * 2 + to_core

    def at_group(shift):
        return (lax.rem(group + shift + groups, groups), dev)

    other = 1 - core
    step = 1 - 2 * core
    half_way = groups // 2

    def any_of(*numbers):
        hit = group == numbers[0]
        for number in numbers[1:]:
            hit = hit | (group == number)
        return hit

    def by_group(table):
        return sum((group == g).astype(jnp.int32) * value for g, value in table.items())

    ways = ({0: 2, 2: 5, 5: 7, 7: 0}, {0: 7, 7: 5, 5: 2, 2: 0})
    sends_far = any_of(0, 2, 5, 7)
    takes_far = any_of(1, 3, 4, 6)
    first_hop = [by_group(way) for way in ways]
    second_hop = [by_group({way[g]: (g + half_way) % groups for g in way}) for way in ways]
    came_from = [by_group({(g + half_way) % groups: way[g] for g in way}) for way in ways]

    barrier = pltpu.get_barrier_semaphore()
    for i, off in enumerate(OFFSETS):
        if i:
            pl.semaphore_signal(barrier, inc=1, device_id=(group, chip_dev(off, 1, core)), device_id_type=MESH)
        pl.semaphore_signal(barrier, inc=1, device_id=(group, chip_dev(off, 1, other)), device_id_type=MESH)
    far_group = lax.rem(group + half_way, groups)
    for i, off in enumerate(OFFSETS):
        for to_core in (core, other):
            pl.semaphore_signal(barrier, inc=1, device_id=(far_group, chip_dev(off, 1, to_core)), device_id_type=MESH)
    for shift in (1, -1):
        pl.semaphore_signal(barrier, inc=1, device_id=at_group(shift), device_id_type=MESH)

    @pl.when(sends_far)
    def _():
        for way in range(2):
            pl.semaphore_signal(barrier, inc=1, device_id=(first_hop[way], dev), device_id_type=MESH)
            pl.semaphore_signal(barrier, inc=2, device_id=(second_hop[way], dev), device_id_type=MESH)

    @pl.when(takes_far)
    def _():
        for way in range(2):
            pl.semaphore_signal(barrier, inc=1, device_id=(came_from[way], dev), device_id_type=MESH)

    values = emb_ref[...].astype(jnp.float32)
    unit[...] = (values * lax.rsqrt(jnp.sum(values * values, axis=1, keepdims=True) + 1e-06)).astype(jnp.bfloat16)

    assign = assign_ref[...]
    ids = lax.broadcasted_iota(jnp.int32, (32, rows), 0)
    owner = jnp.zeros((1, rows), jnp.int32)
    for n in range(owner_of_ref.shape[0]):
        owner = jnp.where(assign == n, owner_of_ref[n], owner)
    index = jnp.full((1, rows), -1, jnp.int32)
    for i, off in enumerate(OFFSETS):
        for q, to_core in enumerate((core, other)):
            index = jnp.where(owner == chip_dev(off, 1, to_core), 2 * i + q, index)
    chosen = (index == ids).astype(jnp.float32)
    before = (lax.broadcasted_iota(jnp.int32, (128, 128), 0)
              < lax.broadcasted_iota(jnp.int32, (128, 128), 1)).astype(jnp.float32).astype(jnp.bfloat16)
    blocks = [chosen[:, n * 128:(n + 1) * 128] for n in range(rows // 128)]
    counted = jnp.dot(jnp.concatenate(blocks, axis=0).astype(jnp.bfloat16), before, preferred_element_type=jnp.float32)
    earlier = jnp.zeros((32, 1), jnp.float32)
    slots = []
    for n, block in enumerate(blocks):
        inside = counted[n * 32:(n + 1) * 32, :] + earlier
        slots.append(jnp.sum(inside * block, axis=0, keepdims=True))
        earlier = earlier + jnp.sum(block, axis=1, keepdims=True)
    slot = jnp.concatenate(slots, axis=1).astype(jnp.int32)
    above = (lax.broadcasted_iota(jnp.int32, (32, 32), 1)
             < lax.broadcasted_iota(jnp.int32, (32, 32), 0)).astype(jnp.float32).astype(jnp.bfloat16)
    base_out[...] = jnp.dot(
        above, jnp.broadcast_to(earlier, (32, 128)).astype(jnp.bfloat16), preferred_element_type=jnp.float32)

    piece = rows // (2 * PIECES)

    def raw_copy(way, k):
        return pltpu.make_async_remote_copy(
            src_ref=in_order.at[pl.ds((2 * k + way) * piece, piece)], dst_ref=relayed.at[way, k],
            send_sem=raw_ss.at[way, k], recv_sem=raw_rs.at[way, k],
            device_id=(first_hop[way], dev), device_id_type=MESH)

    def hop_copy(way, k):
        return pltpu.make_async_remote_copy(
            src_ref=relayed.at[way, k], dst_ref=unit_in.at[pl.ds((2 * k + way) * piece, piece)],
            send_sem=hop_ss.at[way, k], recv_sem=hop_rs.at[way, k],
            device_id=(second_hop[way], dev), device_id_type=MESH)

    base_copy = pltpu.make_async_remote_copy(
        src_ref=base_out, dst_ref=base_in, send_sem=base_sem.at[0], recv_sem=base_sem.at[1],
        device_id=at_group(half_way), device_id_type=MESH)

    def set_hits(index, slot):
        position = lax.broadcasted_iota(jnp.int32, (CHIPS * cap, rows), 0)
        for q, into in enumerate((hits_same, hits_other)):
            place = jnp.where(index % 2 == q, index // 2 * cap + slot, -1)
            into[...] = (place == position).astype(jnp.float32).astype(jnp.bfloat16)

    def packed(hits, source, part, depth):
        some = hits[part[0] * cap:part[1] * cap, 0:depth]
        live = jnp.sum(some.astype(jnp.float32), axis=1, keepdims=True)
        got = jnp.dot(some, source[0:depth, :], preferred_element_type=jnp.float32)
        lane = lax.broadcasted_iota(jnp.int32, got.shape, 1)
        return jnp.where((lane == 0) & (live < 0.5), MARK, got)

    def sib_copy(turn, n):
        first, last = PARTS[turn][n]
        here = pl.ds(first * cap, (last - first) * cap)
        return pltpu.make_async_remote_copy(
            src_ref=sib_out.at[turn, here], dst_ref=sib_in.at[turn, here],
            send_sem=sib_ss.at[turn, n], recv_sem=sib_rs.at[turn, n],
            device_id=(group, chip_dev((0, 0), 1, other)), device_id_type=MESH)

    def chunk_copy(turn, i):
        here = pl.ds(i * chunk, chunk)
        return pltpu.make_async_remote_copy(
            src_ref=outbox.at[turn, here], dst_ref=(members, far)[turn].at[here],
            send_sem=a2a_ss.at[turn, i], recv_sem=a2a_rs.at[turn, i],
            device_id=(group, chip_dev(OFFSETS[i], 1, core)), device_id_type=MESH)

    def give_sibling(turn, source, n, depth=rows):
        part = PARTS[turn][n]
        sib_out[turn, part[0] * cap:part[1] * cap, :] = packed(hits_other, source, part, depth).astype(jnp.bfloat16)
        sib_copy(turn, n).start()

    def make_part(turn, source, n, depth=rows):
        part = PARTS[turn][n]
        own = packed(hits_same, source, part, depth)
        sib_copy(turn, n).wait()
        from_sib = sib_in[turn, part[0] * cap:part[1] * cap, :].astype(jnp.float32)
        for i in range(*part):
            here = slice((i - part[0]) * cap, (i - part[0] + 1) * cap)
            both = jnp.concatenate([own[here, :], from_sib[here, :]], axis=0).astype(jnp.bfloat16)
            if i == 0:
                (members, far)[turn][0:chunk, :] = both
            else:
                outbox[turn, i * chunk:(i + 1) * chunk, :] = both

    def send_part(turn, n):
        for i in range(*PARTS[turn][n]):
            if i:
                chunk_copy(turn, i).start()

    def send_all(turn, source, first):
        last = len(PARTS[turn])
        for n in range(first, min(first + 2, last)):
            give_sibling(turn, source, n)
        for n in range(first, last):
            make_part(turn, source, n)
            send_part(turn, n)
            if n + 2 < last:
                give_sibling(turn, source, n + 2)

    pl.semaphore_wait(barrier, 4 * CHIPS - 1 + 2 + 4)

    @pl.when(sends_far)
    def _():
        base_copy.start()
        sorted_at = jnp.sum(chosen * base_out[:, 0:1], axis=0, keepdims=True).astype(jnp.int32) + slot
        sent = 0
        for n in range(2):
            here = slice(n * rows // 2, (n + 1) * rows // 2)
            position = lax.broadcasted_iota(jnp.int32, (rows // 2, rows), 0) + n * rows // 2
            order = (sorted_at == position).astype(jnp.float32).astype(jnp.bfloat16)
            in_order[here, :] = jnp.dot(order, unit[...], preferred_element_type=jnp.float32).astype(jnp.bfloat16)
            while sent < AHEAD and (sent + 1) * 2 * piece <= (n + 1) * rows // 2:
                for way in range(2):
                    raw_copy(way, sent).start()
                sent += 1

    set_hits(index, slot)
    send_all(0, unit, 0)
    flags[...] = jnp.where(lax.broadcasted_iota(jnp.int32, (8, 128), 0) == 0, pair_ref[0, 0], pair_ref[0, 1]).astype(jnp.float32)
    flag_copies = []
    for n, shift in enumerate((-1, half_way)):
        copy = pltpu.make_async_remote_copy(
            src_ref=flags, dst_ref=flags_in.at[n], send_sem=flag_ss.at[n], recv_sem=flag_rs.at[n],
            device_id=at_group(shift), device_id_type=MESH)
        copy.start()
        flag_copies.append(copy)

    def near_copy(i):
        here = pl.ds(i * chunk, chunk)
        return pltpu.make_async_remote_copy(
            src_ref=members.at[here], dst_ref=near.at[here], send_sem=near_ss.at[i], recv_sem=near_rs.at[i],
            device_id=at_group(step), device_id_type=MESH)

    @pl.when(takes_far)
    def _():
        base_copy.wait_recv()
        base = base_in[:, 0:1].astype(jnp.int32)
        position = lax.broadcasted_iota(jnp.int32, (32, rows), 1)
        begun = base <= position
        far_index = jnp.sum(jnp.where(begun, 1, 0), axis=0, keepdims=True) - 1
        far_slot = position[0:1, :] - jnp.max(jnp.where(begun, base, 0), axis=0, keepdims=True)
        set_hits(far_index, far_slot)

    def send_near(table, k):
        for i in range(table[k - 1] if k else 0, table[k] if k < PIECES else CHIPS):
            if i:
                chunk_copy(0, i).wait_recv()
            near_copy(i).start()

    for k in range(PIECES):
        @pl.when(sends_far)
        def _(k=k):
            for way in range(2):
                raw_copy(way, k).wait_recv()
                hop_copy(way, k).start()
                if k + AHEAD < PIECES:
                    raw_copy(way, k + AHEAD).start()
            send_near(NEAR_SENDER, k)

        @pl.when(takes_far)
        def _(k=k):
            for way in range(2):
                hop_copy(way, k).wait_recv()
            if k + 1 in EARLY:
                give_sibling(1, unit_in, EARLY.index(k + 1), (k + 1) * 2 * piece)
            if k in EARLY:
                make_part(1, unit_in, EARLY.index(k), k * 2 * piece)
                send_part(1, EARLY.index(k))
            send_near(NEAR_TAKER, k)

    @pl.when(sends_far)
    def _():
        send_near(NEAR_SENDER, PIECES)

    @pl.when(takes_far)
    def _():
        send_near(NEAR_TAKER, PIECES)
        send_all(1, unit_in, len(EARLY))

    tiles = 4
    height = total // tiles
    per_tile = CHIPS // tiles
    first_lane = (lax.broadcasted_iota(jnp.int32, (8, 128), 1) == 0).astype(jnp.float32).astype(jnp.bfloat16)
    marks = lax.dot_general(first_lane, members[:, 0:128], (((1,), (1,)), ((), ())), preferred_element_type=jnp.float32)
    col_bias = jnp.where(marks[0:1, :] > 2.0, DEAD, 0.0)

    def product(block, t, kept, column_best):
        self_block = kept is None
        left_at = pl.ds(t * height if isinstance(t, int) else pl.multiple_of(t * height, height), height)
        left = block[left_at, :]
        row_bias = jnp.where(block[left_at, 0:128].astype(jnp.float32)[:, 0:1] > 2.0, DEAD, 0.0)
        row_bias = jnp.broadcast_to(row_bias, (height, COLS))
        lane_best = None
        for n in range(total // COLS):
            cols = slice(n * COLS, (n + 1) * COLS)
            sim = lax.dot_general(left, members[cols, :], (((1,), (1,)), ((), ())), preferred_element_type=jnp.float32)
            down = sim + row_bias
            if self_block:
                row_id = t * height + lax.broadcasted_iota(jnp.int32, (height, COLS), 0)
                col_id = n * COLS + lax.broadcasted_iota(jnp.int32, (height, COLS), 1)
                down = jnp.where(row_id == col_id, DEAD, down)
            else:
                across = sim + col_bias[:, cols]
                across = jnp.maximum(across[:, 0:128], across[:, 128:256])
                lane_best = across if lane_best is None else jnp.maximum(lane_best, across)
            down = jnp.max(down.reshape(height // 8, 8, COLS), axis=0)
            column_best[:, cols] = jnp.maximum(column_best[:, cols], down)
        if not self_block:
            kept[left_at, :] = lane_best

    def fold(kept, into, t):
        for b in range(t * height // 128, (t + 1) * height // 128):
            lanes = slice(b * 128, (b + 1) * 128)
            into[:, lanes] = jnp.max(kept[lanes, :].T, axis=0, keepdims=True)

    best[...] = jnp.full(best.shape, DEAD, jnp.float32)

    def own_tile(t, carry):
        product(members, t, None, best.at[0])
        return carry

    lax.fori_loop(0, tiles, own_tile, 0)

    for copy in flag_copies:
        copy.wait()
    near_on = jnp.where(core == 0, flags[0:1, 0:1], flags_in[0, 0:1, 0:1])
    far_on = jnp.maximum(flags[1:2, 0:1], flags_in[1, 1:2, 0:1])

    near_back = pltpu.make_async_remote_copy(
        src_ref=back_out.at[0], dst_ref=back_in, send_sem=back_sem.at[0], recv_sem=back_sem.at[1],
        device_id=at_group(-step), device_id_type=MESH)

    def ret_copy(turn, j):
        off, to_core = OFFSETS[j // 2], (core, other)[j % 2]
        to_group = lax.rem(group + half_way, groups) if turn else group
        return pltpu.make_async_remote_copy(
            src_ref=ret_out.at[turn, j], dst_ref=ret_in.at[turn, j], send_sem=ret_ss.at[turn, j], recv_sem=ret_rs.at[turn, j],
            device_id=(to_group, chip_dev(off, -1, to_core)), device_id_type=MESH)

    ret_out[...] = jnp.zeros(ret_out.shape, jnp.float32)

    for t in range(tiles):
        for i in range(t * per_tile, (t + 1) * per_tile):
            near_copy(i).wait_recv()
        product(near, t, partial.at[0], best.at[1])
        fold(partial.at[0], back_out.at[0], t)
        if t == tiles - 1:
            back_out[0] = jnp.where(near_on > 0.5, back_out[0], -2.0)
            near_back.start()

        @pl.when(takes_far)
        def _(t=t):
            for i in range(max(1, t * per_tile), (t + 1) * per_tile):
                chunk_copy(1, i).wait_recv()
            product(far, t, partial.at[1], best.at[2])
            fold(partial.at[1], back_out.at[1], t)

    @pl.when(takes_far)
    def _():
        theirs = jnp.where(far_on > 0.5, back_out[1], -2.0)
        for j in range(2 * CHIPS):
            ret_out[1, j, 0:1, 0:cap] = theirs[:, j * cap:(j + 1) * cap]
            ret_copy(1, j).start()
        ret_in[1] = jnp.full(ret_in.shape[1:], -2.0, jnp.float32)

    near_back.wait_recv()
    leading = jnp.maximum(jnp.max(best[0], axis=0, keepdims=True), -1.0)
    leading = jnp.maximum(leading, jnp.where(near_on > 0.5, jnp.max(best[1], axis=0, keepdims=True), -2.0))
    leading = jnp.maximum(leading, jnp.where(far_on > 0.5, jnp.max(best[2], axis=0, keepdims=True), -2.0))
    leading = jnp.maximum(leading, back_in[...])

    for j in range(2 * CHIPS):
        ret_out[0, j, 0:1, 0:cap] = leading[:, j * cap:(j + 1) * cap]
        if j:
            ret_copy(0, j).start()
    ret_in[0, 0] = ret_out[0, 0]

    wanted = chosen.astype(jnp.bfloat16)
    for j in range(1, 2 * CHIPS):
        ret_copy(0, j).wait_recv()

    @pl.when(sends_far)
    def _():
        for j in range(2 * CHIPS):
            ret_copy(1, j).wait_recv()

    got = jnp.maximum(ret_in[0, :, 0, :], ret_in[1, :, 0, :])
    spread = jnp.zeros((128, rows), jnp.float32)
    for _ in range(3):
        part = got.astype(jnp.bfloat16)
        got = got - part.astype(jnp.float32)
        spread = spread + lax.dot_general(part, wanted, (((0,), (0,)), ((), ())), preferred_element_type=jnp.float32)
    pick = lax.broadcasted_iota(jnp.int32, (128, rows), 0) == slot
    out_ref[...] = jnp.sum(jnp.where(pick, spread, 0.0), axis=0, keepdims=True)

    near_back.wait_send()
    for j in range(1, 2 * CHIPS):
        ret_copy(0, j).wait_send()
    for i in range(CHIPS):
        near_copy(i).wait_send()
        if i:
            chunk_copy(0, i).wait_send()

    @pl.when(sends_far)
    def _():
        for k in range(PIECES):
            for way in range(2):
                raw_copy(way, k).wait_send()
                hop_copy(way, k).wait_send()
        base_copy.wait_send()

    @pl.when(takes_far)
    def _():
        for i in range(1, CHIPS):
            chunk_copy(1, i).wait_send()
        for j in range(2 * CHIPS):
            ret_copy(1, j).wait_send()


def on_device(embeddings, assignment, owner_of, pair_on):
    rows, width = embeddings.shape
    owners = owner_of.shape[0]
    cap = 2 * rows // owners
    total = owners * cap
    half = total // 2
    bf16, f32 = jnp.bfloat16, jnp.float32
    dma = pltpu.SemaphoreType.DMA
    out = pl.pallas_call(
        functools.partial(kernel, cap),
        out_shape=jax.ShapeDtypeStruct((1, rows), f32),
        in_specs=[pl.BlockSpec(memory_space=pltpu.VMEM)] * 2 + [pl.BlockSpec(memory_space=pltpu.SMEM)] * 2,
        out_specs=pl.BlockSpec(memory_space=pltpu.VMEM),
        scratch_shapes=[
            pltpu.VMEM((rows, width), bf16),
            pltpu.VMEM((rows, width), bf16),
            pltpu.VMEM((half, rows), bf16),
            pltpu.VMEM((half, rows), bf16),
            pltpu.VMEM((2, half, width), bf16),
            pltpu.VMEM((2, half, width), bf16),
            pltpu.VMEM((2, total, width), bf16),
            pltpu.VMEM((total, width), bf16),
            pltpu.VMEM((total, width), bf16),
            pltpu.VMEM((total, width), bf16),
            pltpu.VMEM((owners, 128), f32),
            pltpu.VMEM((2, PIECES, rows // (2 * PIECES), width), bf16),
            pltpu.VMEM((rows, width), bf16),
            pltpu.VMEM((owners, 128), f32),
            pltpu.VMEM((3, 8, total), f32),
            pltpu.VMEM((2, total, 128), f32),
            pltpu.VMEM((2, 1, total), f32),
            pltpu.VMEM((1, total), f32),
            pltpu.VMEM((8, 128), f32),
            pltpu.VMEM((2, 8, 128), f32),
            pltpu.VMEM((2, owners, 1, 128), f32),
            pltpu.VMEM((2, owners, 1, 128), f32),
            dma((2, 6)), dma((2, 6)),
            dma((2, CHIPS)), dma((2, CHIPS)),
            dma((CHIPS,)), dma((CHIPS,)),
            dma((2, PIECES)), dma((2, PIECES)),
            dma((2, PIECES)), dma((2, PIECES)),
            dma((2,)),
            dma((2,)),
            dma((2,)), dma((2,)),
            dma((2, owners)), dma((2, owners)),
        ],
        compiler_params=pltpu.CompilerParams(
            collective_id=0, has_side_effects=True, vmem_limit_bytes=56 * 2**20),
        cost_estimate=pl.CostEstimate(flops=6 * total * total * width, bytes_accessed=2 * rows * width, transcendentals=0),
        name="semdedup",
    )(embeddings, assignment.reshape(1, rows), owner_of, pair_on.reshape(1, 2))
    return out.reshape(rows)


def solution(mesh):
    placed = (P(("group", "dev"), None), P(("group", "dev"), None), P(), P(None, ("group", "dev")))
    return jax.shard_map(
        on_device, mesh=mesh, in_specs=placed, out_specs=P(("group", "dev")), check_vma=False
    )
```

time: 121 us -> 111 us (0.917)
  Pallas kernels: 119 us -> 110 us
    pallas_call x1, Pallas kernels: 119 us -> 110 us  [on_device(): pl.pallas_call(functools.partial(kernel, cap), out_shape=jax.ShapeDtypeSt...]
where the time goes in v3:
time: 111 us
  Pallas kernels  110 us (99%)
  other arithmetic  1.29 us (1%)
    pallas_call x1, Pallas kernels, on_device(): pl.pallas_call(functools.partial(kernel, cap), out_shape=jax.ShapeDtypeSt...  110 us

profile of v3, /device:TPU:1, one launch (start us, length us, event | category | flops | bytes accessed | tf_op | source)
XLA Modules:
  0.0 111.2 jit_solution(3048297301763860826)
XLA Ops:
  0.0 109.9 %semdedup.1 = f32[1,896]{1,0:T(1,128)} custom-call(bf16[896,768]{1,0:T(8,128)(2,1)} %emb_ref.1, s32[1,896]{1,0:T(1,128)} %bitcast.2, s32[32]{0:T(128)} %owner_of_ref.1, s32[1,2]{1,0:T(1,128)} %bitcast.3), custom_call_target="tpu_custom_call" | custom-call | flops 14797504512 | bytes 1376256 | tf_op jit(solution)/shard_map/semdedup/pallas_call | solution.py:431
  110.0 1.3 %reduce = f32[896]{0:T(1024)} reduce(f32[1,896]{1,0:T(1,128)} %semdedup.1, f32[]{:T(128)} %constant.3), dimensions={0}, to_apply=%pallas_call.3.reduce_sub_computation | reduce | bytes 7172 | tf_op jit(solution)/shard_map/semdedup/pallas_call | solution.py:431

commit v4 on v3

--- a/solution.py
+++ b/solution.py
@@ -20,13 +20,13 @@
 PIECES = 7
 AHEAD = 7
 NEAR_SENDER = (0, 0, 0, 0, 0, 0, 0)
-NEAR_TAKER = (0, 0, 6, 9, 12, 16, 16)
+NEAR_TAKER = (0, 0, 0, 0, 6, 11, 16)
 PARTS = (((0, 4), (4, 8), (8, 12), (12, 16)), ((0, 2), (2, 4), (4, 6), (6, 8), (8, 12), (12, 16)))
 EARLY = (2, 4, 6)
 
 
 def kernel(cap, emb_ref, assign_ref, owner_of_ref, pair_ref, out_ref,
-           unit, in_order, hits_other, hits_same, sib_out, sib_in, outbox, members, near, far,
+           unit, in_order, place, sib_out, sib_in, outbox, members, near, far,
            base_out, relayed, unit_in, base_in,
            best, partial, back_out, back_in, flags, flags_in, ret_out, ret_in,
            sib_ss, sib_rs, a2a_ss, a2a_rs, near_ss, near_rs, raw_ss, raw_rs, hop_ss, hop_rs, base_sem,
@@ -139,16 +139,15 @@
         src_ref=base_out, dst_ref=base_in, send_sem=base_sem.at[0], recv_sem=base_sem.at[1],
         device_id=at_group(half_way), device_id_type=MESH)
 
-    def set_hits(index, slot):
-        position = lax.broadcasted_iota(jnp.int32, (CHIPS * cap, rows), 0)
-        for q, into in enumerate((hits_same, hits_other)):
-            place = jnp.where(index % 2 == q, index // 2 * cap + slot, -1)
-            into[...] = (place == position).astype(jnp.float32).astype(jnp.bfloat16)
-
-    def packed(hits, source, part, depth):
-        some = hits[part[0] * cap:part[1] * cap, 0:depth]
-        live = jnp.sum(some.astype(jnp.float32), axis=1, keepdims=True)
-        got = jnp.dot(some, source[0:depth, :], preferred_element_type=jnp.float32)
+    def set_places(turn, index, slot):
+        for q in range(2):
+            place[turn, q] = jnp.where(index % 2 == q, index // 2 * cap + slot, -1)
+
+    def packed(turn, q, source, part, depth):
+        position = lax.broadcasted_iota(jnp.int32, ((part[1] - part[0]) * cap, depth), 0) + part[0] * cap
+        hits = (place[turn, q, :, 0:depth] == position).astype(jnp.float32)
+        live = jnp.sum(hits, axis=1, keepdims=True)
+        got = jnp.dot(hits.astype(jnp.bfloat16), source[0:depth, :], preferred_element_type=jnp.float32)
         lane = lax.broadcasted_iota(jnp.int32, got.shape, 1)
         return jnp.where((lane == 0) & (live < 0.5), MARK, got)
 
@@ -160,21 +159,31 @@
             send_sem=sib_ss.at[turn, n], recv_sem=sib_rs.at[turn, n],
             device_id=(group, chip_dev((0, 0), 1, other)), device_id_type=MESH)
 
-    def chunk_copy(turn, i):
-        here = pl.ds(i * chunk, chunk)
+    cut = -(-chunk // 32) * 16
+
+    def chunk_copy(turn, i, h):
+        here = pl.ds(i * chunk + h * cut, chunk - cut if h else cut)
         return pltpu.make_async_remote_copy(
             src_ref=outbox.at[turn, here], dst_ref=(members, far)[turn].at[here],
-            send_sem=a2a_ss.at[turn, i], recv_sem=a2a_rs.at[turn, i],
+            send_sem=a2a_ss.at[turn, i, h], recv_sem=a2a_rs.at[turn, i, h],
             device_id=(group, chip_dev(OFFSETS[i], 1, core)), device_id_type=MESH)
+
+    def chunk_arrived(turn, i):
+        for h in range(2):
+            chunk_copy(turn, i, h).wait_recv()
+
+    def chunk_left(turn, i):
+        for h in range(2):
+            chunk_copy(turn, i, h).wait_send()
 
     def give_sibling(turn, source, n, depth=rows):
         part = PARTS[turn][n]
-        sib_out[turn, part[0] * cap:part[1] * cap, :] = packed(hits_other, source, part, depth).astype(jnp.bfloat16)
+        sib_out[turn, part[0] * cap:part[1] * cap, :] = packed(turn, 1, source, part, depth).astype(jnp.bfloat16)
         sib_copy(turn, n).start()
 
     def make_part(turn, source, n, depth=rows):
         part = PARTS[turn][n]
-        own = packed(hits_same, source, part, depth)
+        own = packed(turn, 0, source, part, depth)
         sib_copy(turn, n).wait()
         from_sib = sib_in[turn, part[0] * cap:part[1] * cap, :].astype(jnp.float32)
         for i in range(*part):
@@ -185,10 +194,10 @@
             else:
                 outbox[turn, i * chunk:(i + 1) * chunk, :] = both
 
-    def send_part(turn, n):
+    def send_half(turn, n, h):
         for i in range(*PARTS[turn][n]):
             if i:
-                chunk_copy(turn, i).start()
+                chunk_copy(turn, i, h).start()
 
     def send_all(turn, source, first):
         last = len(PARTS[turn])
@@ -196,9 +205,11 @@
             give_sibling(turn, source, n)
         for n in range(first, last):
             make_part(turn, source, n)
-            send_part(turn, n)
+            send_half(turn, n, 0)
             if n + 2 < last:
                 give_sibling(turn, source, n + 2)
+        for n in range(first, last):
+            send_half(turn, n, 1)
 
     pl.semaphore_wait(barrier, 4 * CHIPS - 1 + 2 + 4)
 
@@ -217,7 +228,7 @@
                     raw_copy(way, sent).start()
                 sent += 1
 
-    set_hits(index, slot)
+    set_places(0, index, slot)
     send_all(0, unit, 0)
     flags[...] = jnp.where(lax.broadcasted_iota(jnp.int32, (8, 128), 0) == 0, pair_ref[0, 0], pair_ref[0, 1]).astype(jnp.float32)
     flag_copies = []
@@ -242,12 +253,12 @@
         begun = base <= position
         far_index = jnp.sum(jnp.where(begun, 1, 0), axis=0, keepdims=True) - 1
         far_slot = position[0:1, :] - jnp.max(jnp.where(begun, base, 0), axis=0, keepdims=True)
-        set_hits(far_index, far_slot)
+        set_places(1, far_index, far_slot)
 
     def send_near(table, k):
         for i in range(table[k - 1] if k else 0, table[k] if k < PIECES else CHIPS):
             if i:
-                chunk_copy(0, i).wait_recv()
+                chunk_arrived(0, i)
             near_copy(i).start()
 
     for k in range(PIECES):
@@ -268,7 +279,8 @@
                 give_sibling(1, unit_in, EARLY.index(k + 1), (k + 1) * 2 * piece)
             if k in EARLY:
                 make_part(1, unit_in, EARLY.index(k), k * 2 * piece)
-                send_part(1, EARLY.index(k))
+                for h in range(2):
+                    send_half(1, EARLY.index(k), h)
             send_near(NEAR_TAKER, k)
 
     @pl.when(sends_far)
@@ -354,16 +366,15 @@
         @pl.when(takes_far)
         def _(t=t):
             for i in range(max(1, t * per_tile), (t + 1) * per_tile):
-                chunk_copy(1, i).wait_recv()
+                chunk_arrived(1, i)
             product(far, t, partial.at[1], best.at[2])
             fold(partial.at[1], back_out.at[1], t)
+            for j in range(t * height // 128 * 128 // cap, (t + 1) * height // 128 * 128 // cap):
+                ret_out[1, j, 0:1, 0:cap] = jnp.where(far_on > 0.5, back_out[1, :, j * cap:(j + 1) * cap], -2.0)
+                ret_copy(1, j).start()
 
     @pl.when(takes_far)
     def _():
-        theirs = jnp.where(far_on > 0.5, back_out[1], -2.0)
-        for j in range(2 * CHIPS):
-            ret_out[1, j, 0:1, 0:cap] = theirs[:, j * cap:(j + 1) * cap]
-            ret_copy(1, j).start()
         ret_in[1] = jnp.full(ret_in.shape[1:], -2.0, jnp.float32)
 
     near_back.wait_recv()
@@ -378,7 +389,8 @@
             ret_copy(0, j).start()
     ret_in[0, 0] = ret_out[0, 0]
 
-    wanted = chosen.astype(jnp.bfloat16)
+    wanted = jnp.concatenate([chosen.astype(jnp.bfloat16)] * 3, axis=0)
+    pick = lax.broadcasted_iota(jnp.int32, (128, rows), 0) == slot
     for j in range(1, 2 * CHIPS):
         ret_copy(0, j).wait_recv()
 
@@ -388,13 +400,14 @@
             ret_copy(1, j).wait_recv()
 
     got = jnp.maximum(ret_in[0, :, 0, :], ret_in[1, :, 0, :])
-    spread = jnp.zeros((128, rows), jnp.float32)
+    parts = []
     for _ in range(3):
         part = got.astype(jnp.bfloat16)
         got = got - part.astype(jnp.float32)
-        spread = spread + lax.dot_general(part, wanted, (((0,), (0,)), ((), ())), preferred_element_type=jnp.float32)
-    pick = lax.broadcasted_iota(jnp.int32, (128, rows), 0) == slot
-    out_ref[...] = jnp.sum(jnp.where(pick, spread, 0.0), axis=0, keepdims=True)
+        parts.append(part)
+    spread = lax.dot_general(
+        jnp.concatenate(parts, axis=0), wanted, (((0,), (0,)), ((), ())), preferred_element_type=jnp.float32)
+    out_ref[...] = jnp.sum(jnp.where(pick, spread, 0.0), axis=0)
 
     near_back.wait_send()
     for j in range(1, 2 * CHIPS):
@@ -402,7 +415,7 @@
     for i in range(CHIPS):
         near_copy(i).wait_send()
         if i:
-            chunk_copy(0, i).wait_send()
+            chunk_left(0, i)
 
     @pl.when(sends_far)
     def _():
@@ -415,7 +428,7 @@
     @pl.when(takes_far)
     def _():
         for i in range(1, CHIPS):
-            chunk_copy(1, i).wait_send()
+            chunk_left(1, i)
         for j in range(2 * CHIPS):
             ret_copy(1, j).wait_send()
 
@@ -430,14 +443,13 @@
     dma = pltpu.SemaphoreType.DMA
     out = pl.pallas_call(
         functools.partial(kernel, cap),
-        out_shape=jax.ShapeDtypeStruct((1, rows), f32),
+        out_shape=jax.ShapeDtypeStruct((rows,), f32),
         in_specs=[pl.BlockSpec(memory_space=pltpu.VMEM)] * 2 + [pl.BlockSpec(memory_space=pltpu.SMEM)] * 2,
         out_specs=pl.BlockSpec(memory_space=pltpu.VMEM),
         scratch_shapes=[
             pltpu.VMEM((rows, width), bf16),
             pltpu.VMEM((rows, width), bf16),
-            pltpu.VMEM((half, rows), bf16),
-            pltpu.VMEM((half, rows), bf16),
+            pltpu.VMEM((2, 2, 1, rows), jnp.int32),
             pltpu.VMEM((2, half, width), bf16),
             pltpu.VMEM((2, half, width), bf16),
             pltpu.VMEM((2, total, width), bf16),
@@ -457,7 +469,7 @@
             pltpu.VMEM((2, owners, 1, 128), f32),
             pltpu.VMEM((2, owners, 1, 128), f32),
             dma((2, 6)), dma((2, 6)),
-            dma((2, CHIPS)), dma((2, CHIPS)),
+            dma((2, CHIPS, 2)), dma((2, CHIPS, 2)),
             dma((CHIPS,)), dma((CHIPS,)),
             dma((2, PIECES)), dma((2, PIECES)),
             dma((2, PIECES)), dma((2, PIECES)),
@@ -471,7 +483,7 @@
         cost_estimate=pl.CostEstimate(flops=6 * total * total * width, bytes_accessed=2 * rows * width, transcendentals=0),
         name="semdedup",
     )(embeddings, assignment.reshape(1, rows), owner_of, pair_on.reshape(1, 2))
-    return out.reshape(rows)
+    return out
 
 
 def solution(mesh):

time: 111 us -> 109 us (0.982)
  Pallas kernels: 110 us -> 107 us
  other arithmetic: 1.29 us -> 0 us
  local copies, waits for them, and re-layouts: 0 us -> 1.28 us
    pallas_call x1, Pallas kernels: 110 us -> 107 us  [on_device(): pl.pallas_call(functools.partial(kernel, cap), out_shape=jax.ShapeDtypeSt...]
    pallas_call x1 -> x0, other arithmetic: 1.29 us -> none  [on_device(): pl.pallas_call(functools.partial(kernel, cap), out_shape=jax.ShapeDtypeSt...]
    unnamed x0 -> x1, local copies, waits for them, and re-layouts: none -> 1.28 us
where the time goes in v4:
time: 109 us; the launch traced here: 108 us
  Pallas kernels  107 us (98%)
  local copies, waits for them, and re-layouts  1.28 us (1%)
    pallas_call x1, Pallas kernels, on_device(): pl.pallas_call(functools.partial(kernel, cap), out_shape=jax.ShapeDtypeSt...  107 us

profile of v4, /device:TPU:1, one launch (start us, length us, event | category | flops | bytes accessed | tf_op | source)
XLA Modules:
  0.0 108.4 jit_solution(2408090330615648277)
XLA Ops:
  0.0 107.2 %semdedup.1 = f32[896]{0:T(1024)} custom-call(bf16[896,768]{1,0:T(8,128)(2,1)} %emb_ref.1, s32[1,896]{1,0:T(1,128)} %bitcast.2, s32[32]{0:T(128)} %owner_of_ref.1, s32[1,2]{1,0:T(1,128)} %bitcast.3), custom_call_target="tpu_custom_call" | custom-call | flops 14797504512 | bytes 1376256 | tf_op jit(solution)/shard_map/semdedup/pallas_call | solution.py:444
  107.2 1.3 %copy.6 = f32[896]{0:T(1024)} copy(f32[896]{0:T(1024)} %semdedup.1) | data formatting | bytes 7168

commit v5 on v4

--- a/solution.py
+++ b/solution.py
@@ -74,10 +74,7 @@
         if i:
             pl.semaphore_signal(barrier, inc=1, device_id=(group, chip_dev(off, 1, core)), device_id_type=MESH)
         pl.semaphore_signal(barrier, inc=1, device_id=(group, chip_dev(off, 1, other)), device_id_type=MESH)
-    far_group = lax.rem(group + half_way, groups)
-    for i, off in enumerate(OFFSETS):
-        for to_core in (core, other):
-            pl.semaphore_signal(barrier, inc=1, device_id=(far_group, chip_dev(off, 1, to_core)), device_id_type=MESH)
+    pl.semaphore_signal(barrier, inc=1, device_id=at_group(half_way), device_id_type=MESH)
     for shift in (1, -1):
         pl.semaphore_signal(barrier, inc=1, device_id=at_group(shift), device_id_type=MESH)
 
@@ -86,6 +83,11 @@
         for way in range(2):
             pl.semaphore_signal(barrier, inc=1, device_id=(first_hop[way], dev), device_id_type=MESH)
             pl.semaphore_signal(barrier, inc=2, device_id=(second_hop[way], dev), device_id_type=MESH)
+        far_group = lax.rem(group + half_way, groups)
+        for i, off in enumerate(OFFSETS):
+            for to_core in (core, other):
+                if i or to_core is other:
+                    pl.semaphore_signal(barrier, inc=1, device_id=(far_group, chip_dev(off, 1, to_core)), device_id_type=MESH)
 
     @pl.when(takes_far)
     def _():
@@ -211,7 +213,7 @@
         for n in range(first, last):
             send_half(turn, n, 1)
 
-    pl.semaphore_wait(barrier, 4 * CHIPS - 1 + 2 + 4)
+    pl.semaphore_wait(barrier, 2 * CHIPS - 1 + 1 + 2 + 4 + (2 * CHIPS - 1) * takes_far.astype(jnp.int32))
 
     @pl.when(sends_far)
     def _():
@@ -277,10 +279,9 @@
                 hop_copy(way, k).wait_recv()
             if k + 1 in EARLY:
                 give_sibling(1, unit_in, EARLY.index(k + 1), (k + 1) * 2 * piece)
-            if k in EARLY:
-                make_part(1, unit_in, EARLY.index(k), k * 2 * piece)
+                make_part(1, unit_in, EARLY.index(k + 1), (k + 1) * 2 * piece)
                 for h in range(2):
-                    send_half(1, EARLY.index(k), h)
+                    send_half(1, EARLY.index(k + 1), h)
             send_near(NEAR_TAKER, k)
 
     @pl.when(sends_far)

time: 109 us -> 107 us (0.982)
    pallas_call x1, Pallas kernels: 107 us -> 106 us  [on_device(): pl.pallas_call(functools.partial(kernel, cap), out_shape=jax.ShapeDtypeSt...]
where the time goes in v5:
time: 107 us
  Pallas kernels  106 us (99%)
  local copies, waits for them, and re-layouts  1.28 us (1%)
    pallas_call x1, Pallas kernels, on_device(): pl.pallas_call(functools.partial(kernel, cap), out_shape=jax.ShapeDtypeSt...  106 us

profile of v5, /device:TPU:1, one launch (start us, length us, event | category | flops | bytes accessed | tf_op | source)
XLA Modules:
  0.0 107.0 jit_solution(9425949295299755541)
XLA Ops:
  0.0 105.7 %semdedup.1 = f32[896]{0:T(1024)} custom-call(bf16[896,768]{1,0:T(8,128)(2,1)} %emb_ref.1, s32[1,896]{1,0:T(1,128)} %bitcast.2, s32[32]{0:T(128)} %owner_of_ref.1, s32[1,2]{1,0:T(1,128)} %bitcast.3), custom_call_target="tpu_custom_call" | custom-call | flops 14797504512 | bytes 1376256 | tf_op jit(solution)/shard_map/semdedup/pallas_call | solution.py:445
  105.7 1.3 %copy.6 = f32[896]{0:T(1024)} copy(f32[896]{0:T(1024)} %semdedup.1) | data formatting | bytes 7168
